TPU v7x, 256 devices: a whole 4x4x8 slice. The times are simulated.
256 devices in a mesh: kvseq: 32 (over x, z), kvhead: 8 (over y, core).
Axes of the slice: x: 4, y: 4, z: 8, core: 2. Of those that a mesh axis runs over, the one named last changes fastest.
Arguments:
- residual_input: bfloat16 [8, 16384], P(None, ('kvseq', 'kvhead')), may hold values from -1210 to 1210
- norm_gain_vector: bfloat16 [16384], P(('kvseq', 'kvhead')), may hold values from 0.5 to 2
- query_weight: bfloat16 [16384, 8, 2048], P(None, 'kvhead', 'kvseq'), may hold values from -0.046875 to 0.046875
- key_value_weight: bfloat16 [16384, 8, 256], P('kvseq', 'kvhead'), may hold values from -0.046875 to 0.046875
- output_weight: bfloat16 [8, 2048, 16384], P('kvhead', None, 'kvseq'), may hold values from -0.75 to 0.75
- adapter_down_factors: bfloat16 [8, 16384, 32], P(None, 'kvhead'), may hold values from -0.046875 to 0.046875
- query_up_factors: bfloat16 [8, 16, 8, 2048], P(None, None, 'kvhead', 'kvseq'), may hold values from -1.5 to 1.5
- value_up_factors: bfloat16 [8, 16, 8, 128], P(None, None, 'kvhead'), may hold values from -1.5 to 1.5
- adapter_index: int32 [8], replicated, may hold values from 0 to 7
- lengths: int32 [8], replicated, may hold values from 4096 to 32767, as said below
- rotated_key_cache: bfloat16 [8, 32768, 8, 128], P(None, 'kvseq', 'kvhead'), may hold values from -1208 to 1208
- earlier_value_cache: bfloat16 [8, 32768, 8, 128], P(None, 'kvseq', 'kvhead'), may hold values from -24 to 24
Outputs:
- attn_delta: bfloat16 [8, 16384], P(None, ('kvseq', 'kvhead'))
- new_keyval: bfloat16 [8, 8, 256], P(None, 'kvhead')
Inputs may be any that keep to these rules, and one draw needn't show every extreme that they name: Row b has lengths[b] cached positions, 0 to lengths[b] - 1, and its new token stands at position lengths[b]; some row has exactly 32767.
All inputs are finite; a program needn't handle non-finite values.
Results may differ from a plain program's by a relative error of at most 0.015.
The roundings to bfloat16 on the way count: a program that leaves them out, or rounds other values in their place, can miss the bound.
Values may be sent and summed in bfloat16 or wider, within the bound.
A program may use at most 64 MiB of HBM per device.

v0:
```python
import math

import jax
import jax.numpy as jnp
from jax import lax
from jax.sharding import PartitionSpec as P

MODEL_WIDTH = 16384
HEADS_PER_GROUP = 16
HEAD_SIZE = 128
ADAPTER_RANK = 16
ADAPTER_COUNT = 8


epsilon = 1e-05
rope_base = 500000.0
masked_fill = -1e30


def combined_all(shard, axis, combine):
    everything = jax.tree.map(lambda part: lax.all_gather(part, axis), shard)
    first = jax.tree.map(lambda part: part[0], everything)

    def step(k, so_far):
        return combine(so_far, jax.tree.map(lambda part: part[k], everything))

    return lax.fori_loop(1, lax.axis_size(axis), step, first)


def rotary(vector, position):
    half_dim = vector.shape[-1] // 2
    frequency = jnp.exp(jnp.arange(half_dim, dtype=jnp.float32) * (-math.log(rope_base) / half_dim))
    angles = position * frequency
    cosine = jnp.cos(angles)
    sine_part = jnp.sin(angles)
    former = vector[..., :half_dim]
    latter = vector[..., half_dim:]
    return jnp.concatenate(
        [former * cosine - latter * sine_part, latter * cosine + former * sine_part], axis=-1
    )


def combine_parts(former, latter):
    highest = jnp.maximum(former[0], latter[0])
    weight_a = jnp.exp(former[0] - highest)
    weight_b = jnp.exp(latter[0] - highest)
    return (
        highest,
        former[1] * weight_a + latter[1] * weight_b,
        former[2] * weight_a[..., None] + latter[2] * weight_b[..., None],
    )


def finish_rows(peak_in, summed_in, weighted_in, self_score, own_value):
    highest = jnp.maximum(peak_in, self_score)
    factor = jnp.exp(peak_in - highest)
    self_weight = jnp.exp(self_score - highest)
    return (weighted_in * factor + self_weight * own_value) / (summed_in * factor + self_weight)


def local(
    residual_input,
    norm_gain_vector,
    query_weight,
    key_value_weight,
    output_weight,
    adapter_down_factors,
    query_up_factors,
    value_up_factors,
    adapter_index,
    lengths,
    rotated_key_cache,
    earlier_value_cache,
):
    batch_rows = residual_input.shape[0]
    seq_index = lax.axis_index("kvseq")
    group_index = lax.axis_index("kvhead")
    widened = residual_input.astype(jnp.float32)
    square_sum = lax.psum(jnp.sum(widened * widened, axis=1), ("kvseq", "kvhead"))
    scaling = lax.rsqrt(square_sum[:, None] / MODEL_WIDTH + epsilon)
    normed_part = (widened * scaling * norm_gain_vector.astype(jnp.float32)[None, :]).astype(
        jnp.bfloat16
    )
    normed = lax.all_gather(normed_part, ("kvseq", "kvhead"), axis=1, tiled=True)
    selector = (
        adapter_index[:, None] == jnp.arange(ADAPTER_COUNT, dtype=jnp.int32)[None, :]
    ).astype(jnp.float32)
    grouped_rows = adapter_down_factors.shape[1]
    normalized_input = lax.dynamic_slice_in_dim(normed, group_index * grouped_rows, grouped_rows, 1)
    per_adapter = jnp.einsum(
        "cm,xmj->cxj", normalized_input, adapter_down_factors, preferred_element_type=jnp.float32
    )
    partial_low = jnp.sum(per_adapter * selector[:, :, None], axis=1)
    low_rank = lax.psum(partial_low, "kvhead")
    low_rank = low_rank.astype(jnp.bfloat16)
    query_total_width = query_weight.shape[2]
    query_plain = jnp.dot(
        normed,
        query_weight.reshape(MODEL_WIDTH, query_total_width),
        preferred_element_type=jnp.float32,
    )
    query_coef = (
        selector[:, :, None] * low_rank[:, None, :ADAPTER_RANK].astype(jnp.float32)
    ).astype(jnp.bfloat16)
    query_adapter_delta = jnp.einsum(
        "bar,arf->bf",
        query_coef,
        query_up_factors.reshape(ADAPTER_COUNT, ADAPTER_RANK, query_total_width),
        preferred_element_type=jnp.float32,
    )
    query_portion = (query_plain + query_adapter_delta).astype(jnp.bfloat16)
    query_matrix = lax.all_gather(query_portion, "kvseq", axis=1, tiled=True)
    seq_rows = key_value_weight.shape[0]
    normed_seq = lax.dynamic_slice_in_dim(normed, seq_index * seq_rows, seq_rows, 1)
    keyval_part = jnp.dot(
        normed_seq,
        key_value_weight.reshape(seq_rows, 2 * HEAD_SIZE),
        preferred_element_type=jnp.float32,
    )
    key_value_rows = lax.psum(keyval_part, "kvseq")
    value_coef = (
        selector[:, :, None] * low_rank[:, None, ADAPTER_RANK:].astype(jnp.float32)
    ).astype(jnp.bfloat16)
    value_adapter_delta = jnp.einsum(
        "bar,arh->bh",
        value_coef,
        value_up_factors.reshape(ADAPTER_COUNT, ADAPTER_RANK, HEAD_SIZE),
        preferred_element_type=jnp.float32,
    )
    fresh_value = (key_value_rows[:, HEAD_SIZE:] + value_adapter_delta).astype(jnp.bfloat16)
    position = lengths.astype(jnp.float32)
    key_new = rotary(key_value_rows[:, :HEAD_SIZE], position[:, None]).astype(jnp.bfloat16)
    new_keyval = jnp.concatenate([key_new, fresh_value], axis=1)[:, None, :]
    q_rot = rotary(
        query_matrix.astype(jnp.float32).reshape(batch_rows, HEADS_PER_GROUP, HEAD_SIZE),
        position[:, None, None],
    ).astype(jnp.bfloat16)
    key_rows = rotated_key_cache[:, :, 0, :]
    value_rows = earlier_value_cache[:, :, 0, :]
    span_rows = key_rows.shape[1]
    score_scale = 1.0 / math.sqrt(HEAD_SIZE)
    scores = (
        jnp.einsum("bqh,bph->bqp", q_rot, key_rows, preferred_element_type=jnp.float32)
        * score_scale
    )
    positions = seq_index * span_rows + jnp.arange(span_rows, dtype=jnp.int32)
    is_valid = positions[None, None, :] < lengths[:, None, None]
    masked = jnp.where(is_valid, scores, masked_fill)
    block_max = jnp.max(masked, axis=2)
    weights = jnp.where(is_valid, jnp.exp(masked - block_max[:, :, None]), 0.0)
    block_total = jnp.sum(weights, axis=2)
    block_acc = jnp.einsum(
        "bqp,bph->bqh", weights.astype(jnp.bfloat16), value_rows, preferred_element_type=jnp.float32
    )
    self_score = (
        jnp.einsum("bqh,bh->bq", q_rot, key_new, preferred_element_type=jnp.float32) * score_scale
    )
    peak_all, summed_all, weighted_all = combined_all(
        (block_max, block_total, block_acc), "kvseq", combine_parts
    )
    finished = finish_rows(
        peak_all[:, :, None],
        summed_all[:, :, None],
        weighted_all,
        self_score[:, :, None],
        fresh_value.astype(jnp.float32)[:, None, :],
    )
    attended = finished.reshape(batch_rows, HEADS_PER_GROUP * HEAD_SIZE).astype(jnp.bfloat16)
    out_width = output_weight.shape[2]
    partial_out = jnp.dot(
        attended,
        output_weight.reshape(HEADS_PER_GROUP * HEAD_SIZE, out_width),
        preferred_element_type=jnp.float32,
    )
    attn_delta = lax.psum_scatter(partial_out, "kvhead", scatter_dimension=1, tiled=True).astype(
        jnp.bfloat16
    )
    return (attn_delta, new_keyval)


def solution(mesh):
    return jax.shard_map(
        local,
        mesh=mesh,
        in_specs=(
            P(None, ("kvseq", "kvhead")),
            P(("kvseq", "kvhead")),
            P(None, "kvhead", "kvseq"),
            P("kvseq", "kvhead", None),
            P("kvhead", None, "kvseq"),
            P(None, "kvhead", None),
            P(None, None, "kvhead", "kvseq"),
            P(None, None, "kvhead", None),
            P(),
            P(),
            P(None, "kvseq", "kvhead", None),
            P(None, "kvseq", "kvhead", None),
        ),
        out_specs=(P(None, ("kvseq", "kvhead")), P(None, "kvhead", None)),
        check_vma=False,
    )
```

profile of v0, /device:TPU:1, one launch (start us, length us, event | category | flops | bytes accessed | tf_op | source)
XLA Modules:
  0.0 452.5 jit_solution(4916261242815692657)
XLA Ops:
  7.3 0.9 fusion.47
  8.2 0.7 convert_element_type.61
  8.8 81.4 %psum.21 = f32[8]{0:T(128)S(1)} all-reduce(f32[8]{0:T(128)S(1)} %fusion.47), channel_id=1, replica_groups=mesh['kvseq'=32,'kvhead'=8] {'kvseq','kvhead'}, use_global_device_ids=true, to_apply=%region_1.0 | all-reduce | flops 8 | bytes 64 | tf_op jit(solution)/shard_map/psum | solution.py:79
  90.2 0.7 convert_element_type.68
  90.9 0.7 broadcast_compare_fusion
  91.6 0.7 fusion.53
  92.3 0.8 fusion.54
  93.0 66.3 %all-gather.3 = bf16[256,64,8]{1,2,0:T(8,128)(2,1)S(1)} all-gather(bf16[1,64,8]{1,2,0:T(8,128)(2,1)S(1)} %fusion.54), channel_id=1, replica_groups=mesh['kvseq'=32,'kvhead'=8] {'kvseq','kvhead'}, dimensions={0}, use_global_device_ids=true | all-gather | bytes 263168 | tf_op jit(solution)/shard_map/all_gather | solution.py:84
  159.4 0.5 reshape.189
  159.9 2.0 fusion.20
  161.9 11.9 %psum.22 = bf16[8,32]{1,0:T(8,128)(2,1)S(1)} all-reduce(f32[8,32]{1,0:T(8,128)S(1)} %fusion.20), channel_id=1, replica_groups=mesh['kvseq'=32,'kvhead'=8] {'kvhead'}, use_global_device_ids=true, to_apply=%region_3.0 | all-reduce | flops 256 | bytes 1536 | tf_op jit(solution)/shard_map/psum | solution.py:94
  173.8 2.2 fusion.9
  176.0 0.2 fusion.29
  176.2 59.1 %psum.23 = f32[8,256]{1,0:T(8,128)S(1)} all-reduce(f32[8,256]{1,0:T(8,128)S(1)} %fusion.29), channel_id=1, replica_groups=mesh['kvseq'=32,'kvhead'=8] {'kvseq'}, use_global_device_ids=true, to_apply=%region_8.9 | all-reduce | flops 2048 | bytes 16384 | tf_op jit(solution)/shard_map/psum | solution.py:120
  235.4 0.3 fusion.25
  235.7 33.8 %all-gather.4 = bf16[32,64,8]{1,2,0:T(8,128)(2,1)S(1)} all-gather(bf16[1,64,8]{1,2,0:T(8,128)(2,1)S(1)} %fusion.25), channel_id=1, replica_groups=mesh['kvseq'=32,'kvhead'=8] {'kvseq'}, dimensions={0}, use_global_device_ids=true | all-gather | bytes 33792 | tf_op jit(solution)/shard_map/all_gather | solution.py:112
  269.6 0.1 subtract_convert_fusion.1
  269.9 0.8 fusion.63
  270.6 0.6 copy-done.1
  271.2 1.1 fusion.5
  272.4 33.7 %all-gather = f32[256,16]{1,0:T(8,128)S(1)} all-gather(f32[8,16]{1,0:T(8,128)S(1)} %get-tuple-element.212), channel_id=2, replica_groups=mesh['kvseq'=32,'kvhead'=8] {'kvseq'}, dimensions={0}, use_global_device_ids=true | all-gather | bytes 16896 | tf_op jit(solution)/shard_map/all_gather | solution.py:21
  306.0 0.2 fusion.27
  306.3 32.2 %all-gather.1 = f32[256,16]{1,0:T(8,128)S(1)} all-gather(f32[8,16]{1,0:T(8,128)S(1)} %fusion.27), channel_id=3, replica_groups=mesh['kvseq'=32,'kvhead'=8] {'kvseq'}, dimensions={0}, use_global_device_ids=true | all-gather | bytes 16896 | tf_op jit(solution)/shard_map/all_gather | solution.py:21
  338.6 0.2 fusion.46
  338.8 0.3 fusion.64
  339.0 28.7 %all-gather.7.cloned.1.call-done = f32[256,16,128]{2,1,0:T(8,128)} async-done(((f32[8,16,128]{2,1,0:T(8,128)}), f32[256,16,128]{2,1,0:T(8,128)}) %all-gather.7.cloned.1.call-update) | async-done | bytes 2097168 | tf_op jit(solution)/shard_map/all_gather | solution.py:21
  367.8 0.8 slice.50
  368.6 31.2 %while.19 = (s32[]{:T(128)}, f32[8,16]{1,0:T(8,128)S(1)}, f32[8,16]{1,0:T(8,128)S(1)}, f32[8,16,128]{2,1,0:T(8,128)S(1)}, f32[32,8,16]{2,1,0:T(8,128)S(1)}, /*in...) while((s32[]{:T(128)}, f32[8,16]{1,0:T(8,128)S(1)}, ...), condition=%wide.region_7.8_spmd, body=%wide.region_6.7_spmd.sunk | while | flops 49925 | bytes 201871 | solution.py:27
  368.6 1.0 fusion.70
  369.6 1.0 fusion.70
  370.6 1.0 fusion.70
  371.6 1.0 fusion.70
  372.6 1.0 fusion.70
  373.6 1.0 fusion.70
  374.6 1.0 fusion.70
  375.7 1.0 fusion.70
  376.7 1.0 fusion.70
  377.7 1.0 fusion.70
  378.7 1.0 fusion.70
  379.7 1.0 fusion.70
  380.7 1.0 fusion.70
  381.7 1.0 fusion.70
  382.7 1.0 fusion.70
  383.7 1.0 fusion.70
  384.7 1.0 fusion.70
  385.7 1.0 fusion.70
  386.7 1.0 fusion.70
  387.7 1.0 fusion.70
  388.7 1.0 fusion.70
  389.7 1.0 fusion.70
  390.8 1.0 fusion.70
  391.8 1.0 fusion.70
  392.8 1.0 fusion.70
  393.8 1.0 fusion.70
  394.8 1.0 fusion.70
  395.8 1.0 fusion.70
  396.8 1.0 fusion.70
  397.8 1.0 fusion.70
  398.8 1.0 fusion.70
  399.8 0.1 fusion.40
  399.9 3.2 fusion.17
  403.2 0.7 maximum_bitcast_fusion
  403.8 40.4 %reduce-scatter.4.cloned.1.call-done = f32[64,8]{1,0:T(8,128)} async-done(((f32[512,8]{1,0:T(8,128)}), f32[64,8]{1,0:T(8,128)}) %reduce-scatter.4.cloned.1.call-update) | async-done | bytes 2064
  444.2 1.4 copy.22
  (57 shorter events, 1.2 us)
Async XLA Ops:
  7.2 262.7 %copy-start = (bf16[8,1024,1,128]{3,1,2,0:T(8,128)(2,1)S(1)}, bf16[8,1024,1,128]{3,1,2,0:T(8,128)(2,1)}, u32[]{:S(2)}) copy-start(bf16[8,1024,1,128]{3,1,2,0:T(8,128)(2,1)} %param.24) | copy-start | bytes 6291460
  7.2 360.6 %all-gather.7.cloned.1.call-start = ((), (), s32[]{:S(2)}) async-start(), calls=%async_computation.1 | async-start | bytes 2162688 | tf_op jit(solution)/shard_map/all_gather | solution.py:21
  159.4 16.7 %copy-start.2 = (bf16[512,1,256]{2,0,1:T(8,128)(2,1)S(1)}, bf16[512,1,256]{2,0,1:T(8,128)(2,1)}, u32[]{:S(2)}) copy-start(bf16[512,1,256]{2,0,1:T(8,128)(2,1)} %param.17) | copy-start | bytes 786436
  159.4 76.0 %copy-start.3 = (bf16[8,16,1,64]{3,1,2,0:T(8,128)(2,1)S(1)}, bf16[8,16,1,64]{3,1,2,0:T(8,128)(2,1)}, u32[]{:S(2)}) copy-start(bf16[8,16,1,64]{3,1,2,0:T(8,128)(2,1)} %param.20) | copy-start | bytes 49156
  269.6 1.6 copy-start.1
  270.6 68.1 %copy-start.4 = (bf16[8,16,1,128]{3,1,2,0:T(8,128)(2,1)S(1)}, bf16[8,16,1,128]{3,1,2,0:T(8,128)(2,1)}, u32[]{:S(2)}) copy-start(bf16[8,16,1,128]{3,1,2,0:T(8,128)(2,1)} %param.21) | copy-start | bytes 98308
  272.3 171.9 %reduce-scatter.4.cloned.1.call-start = ((), (), s32[]{:S(2)}) async-start(), calls=%async_computation.2 | async-start | bytes 294912
Sparse Core Ops, SparseCore 0:
  272.4 95.2 all-gather.6
  403.3 40.8 reduce-scatter.3
where the time goes:
time: 456 us; the launch traced here: 452 us
  blocking collectives  318 us (70%)
  waiting for transfers between devices  69.1 us (15%)
  other arithmetic  36 us (8%)
  between operations  14.2 us (3%)
  matrix products  10.2 us (2%)
    psum x1, blocking collectives, local(): lax.psum(jnp.sum(widened * widened, axis=1), ('kvseq', 'kvhead'))  81.4 us
    all_gather x1, blocking collectives, local(): lax.all_gather(normed_part, ('kvseq', 'kvhead'), axis=1, tiled=True)  66.3 us
    all_gather x2, blocking collectives, combined_all(): everything = jax.tree.map(lambda part: lax.all_gather(part, axis), shard)  65.9 us
    psum x1, blocking collectives, local(): key_value_rows = lax.psum(keyval_part, 'kvseq')  59.1 us
    unnamed x3, waiting for transfers between devices  40.4 us
    all_gather x1, blocking collectives, local(): query_matrix = lax.all_gather(query_portion, 'kvseq', axis=1, tiled=True)  33.8 us
    add x31, other arithmetic, combine_parts(): former[2] * weight_a[..., None] + latter[2] * weight_b[..., None]  29.6 us
    all_gather x1, waiting for transfers between devices, combined_all(): everything = jax.tree.map(lambda part: lax.all_gather(part, axis), shard)  28.7 us
  transfers between devices with their start and end apart: 2, of which 2 were waited for; matrix products, arithmetic and copies ran while one was open for 0% of the time, Pallas kernels for 0%

commit v1 on v0

v1 whole, which is shorter than its diff:
```python
import math

import jax
import jax.numpy as jnp
import numpy as np
from jax import lax
from jax.experimental import pallas as pl
from jax.experimental.pallas import tpu as pltpu
from jax.sharding import PartitionSpec as P

MODEL_WIDTH = 16384
HEADS = 16
HEAD_SIZE = 128
HALF = HEAD_SIZE // 2
ADAPTERS = 8
RANK = 16
ROWS = 8
SPAN = 1024
NX, NY, NZ, NC = 4, 4, 8, 2
SEQ = NX * NZ
GROUPS = NY * NC
QUADS = SEQ // ROWS

EPSILON = 1e-05
ROPE_BASE = 500000.0
MASKED = -1e30
SCORE_SCALE = 1.0 / math.sqrt(HEAD_SIZE)
MESH = pl.DeviceIdType.MESH
F32 = jnp.float32
BF16 = jnp.bfloat16
NT = (((1,), (1,)), ((), ()))


def ring(k, n):
    return min(k, n - k)


def offsets(xs, ys, zs, cs):
    found = [(x, y, z, c) for x in xs for y in ys for z in zs for c in cs if (x, y, z, c) != (0, 0, 0, 0)]
    return sorted(found, key=lambda o: (-(ring(o[0], NX) + ring(o[1], NY) + ring(o[2], NZ)), -o[3]))


Z_PARTNERS = offsets([0], [0], range(NZ), range(NC))
XY_PARTNERS = offsets(range(NX), range(NY), [0], [0])
HEAD_PARTNERS = offsets([0], range(NY), [0], range(NC))
SEQ_PARTNERS = offsets(range(NX), [0], range(NZ), [0])


def kernel(
    x_hbm, gain_hbm, qw_hbm, kvw_hbm, ow_hbm, down_hbm, qup_hbm, vup_hbm, adapter_hbm, length_hbm, k_hbm, v_hbm, freq_hbm,
    out_ref, kv_ref,
    x_v, gain_v, qw_v, kvw_v, ow_v, down_v, qup_v, vup_v, adapter_s, length_s, k_v, v_v, freq_v,
    z_msg, z_buf, xy_buf, normed, b_buf, c_msg, c_buf, q_rot, d_msg, d_buf, kv_rows, e_buf, f_msg, f_buf,
    local_sem, send_sem, recv_sem,
):
    seq, head = lax.axis_index("kvseq"), lax.axis_index("kvhead")
    x, z = seq // NZ, lax.rem(seq, NZ)
    y, c = head // NC, lax.rem(head, NC)

    def place(o):
        px, pz = lax.rem(x + o[0], NX), lax.rem(z + o[2], NZ)
        py, pc = lax.rem(y + o[1], NY), lax.rem(c + o[3], NC)
        return px * NZ + pz, py * NC + pc

    barrier = pltpu.get_barrier_semaphore()
    for o in XY_PARTNERS + Z_PARTNERS:
        pl.semaphore_signal(barrier, inc=1, device_id=place(o), device_id_type=MESH)

    fetches = {}
    for n, (name, src, dst) in enumerate([
        ("x", x_hbm, x_v), ("gain", gain_hbm, gain_v), ("adapter", adapter_hbm, adapter_s), ("length", length_hbm, length_s),
        ("freq", freq_hbm, freq_v), ("down", down_hbm, down_v), ("qw", qw_hbm, qw_v), ("kvw", kvw_hbm, kvw_v),
        ("qup", qup_hbm, qup_v.at[:, pl.ds(0, RANK)]), ("vup", vup_hbm, vup_v.at[:, pl.ds(RANK, RANK)]),
        ("k", k_hbm, k_v), ("v", v_hbm, v_v), ("ow", ow_hbm, ow_v),
    ]):
        fetches[name] = pltpu.make_async_copy(src, dst, local_sem.at[n])
        fetches[name].start()

    sent = []

    def send(phase, o, src, dst):
        copy = pltpu.make_async_remote_copy(
            src_ref=src, dst_ref=dst, send_sem=send_sem.at[phase], recv_sem=recv_sem.at[phase],
            device_id=place(o), device_id_type=MESH,
        )
        copy.start()

    def landed(phase, ref, sem=None):
        pltpu.make_async_copy(ref, ref, recv_sem.at[phase]).wait()
        sent.append((phase, ref))

    lane = lax.broadcasted_iota(jnp.int32, (ROWS, 128), 1)
    sub = lax.broadcasted_iota(jnp.int32, (ROWS, 128), 0)

    fetches["x"].wait()
    fetches["gain"].wait()
    mine = x_v[...].astype(F32)
    gains = jnp.broadcast_to(gain_v[...].astype(F32).reshape(1, HALF), (ROWS, HALF))
    both = jnp.concatenate([mine, jnp.where(sub[:, :HALF] == 0, gains, 0.0)], axis=0)
    both = jnp.concatenate([both, both], axis=1)
    lane2 = lax.broadcasted_iota(jnp.int32, (2 * ROWS, 128), 1)
    block = jnp.where(lane2 // HALF == c, both, 0.0).astype(BF16)
    z_msg[...] = block
    z_buf[pl.ds(z * NC + c, 1)] = block[None]

    pl.semaphore_wait(barrier, len(XY_PARTNERS) + len(Z_PARTNERS))
    for o in Z_PARTNERS:
        send(0, o, z_msg, z_buf.at[z * NC + c])

    fetches["length"].wait()
    fetches["freq"].wait()
    fetches["adapter"].wait()
    position = jnp.zeros((ROWS, 128), F32)
    adapter = jnp.zeros((ROWS, ADAPTERS * 2 * RANK), jnp.int32)
    sub_wide = lax.broadcasted_iota(jnp.int32, adapter.shape, 0)
    for b in range(ROWS):
        position = jnp.where(sub == b, length_s[b].astype(F32), position)
        adapter = jnp.where(sub_wide == b, adapter_s[b], adapter)
    chosen = adapter == lax.broadcasted_iota(jnp.int32, adapter.shape, 1) // (2 * RANK)
    angles = position * freq_v[...]
    cosine, sine = jnp.cos(angles), jnp.sin(angles)
    qup_v[:, RANK:, :] = jnp.zeros((ADAPTERS, RANK, HALF), BF16)
    vup_v[:, :RANK, :] = jnp.zeros((ADAPTERS, RANK, HEAD_SIZE), BF16)

    landed(0, z_buf.at[pl.ds(0, NZ * NC - 1)])
    tiles = [z_buf[2 * k].astype(F32) + z_buf[2 * k + 1].astype(F32) for k in range(NZ)]
    packed = [jnp.concatenate([tiles[k][:ROWS], tiles[k + 1][:ROWS]], axis=0) for k in range(0, NZ, 2)]
    gain_rows = jnp.zeros((2 * ROWS, 128), F32)
    sub2 = lax.broadcasted_iota(jnp.int32, gain_rows.shape, 0)
    for k in range(NZ):
        gain_rows = jnp.where(sub2 == k, tiles[k][ROWS : ROWS + 1], gain_rows)
    xy_mine = xy_buf.at[x * NY + y]
    xy_mine[...] = jnp.concatenate(packed + [gain_rows], axis=0).astype(BF16)
    for o in XY_PARTNERS:
        send(1, o, xy_mine, xy_mine)
    landed(1, xy_buf.at[pl.ds(0, NX * NY - 1)])

    squares = jnp.zeros((2 * ROWS, 128), F32)
    for k in range(NX * NY):
        for p in range(NZ // 2):
            part = xy_buf[k, pl.ds(2 * ROWS * p, 2 * ROWS)].astype(F32)
            squares = squares + part * part
    square_sum = jnp.sum(squares[:ROWS] + squares[ROWS:], axis=1, keepdims=True)
    scaling = jnp.broadcast_to(lax.rsqrt(square_sum / MODEL_WIDTH + EPSILON), (ROWS, 128))
    scaling = jnp.concatenate([scaling, scaling], axis=0)
    for k in range(NX * NY):
        kx, ky = k // NY, k % NY
        gain_k = xy_buf[k, pl.ds(NZ * ROWS, 2 * ROWS)].astype(F32)
        for p in range(NZ // 2):
            part = xy_buf[k, pl.ds(2 * ROWS * p, 2 * ROWS)].astype(F32) * scaling
            for i in range(2):
                kz = 2 * p + i
                tile = (kx * NZ + kz) * NY + ky
                normed[:, pl.ds(tile * 128, 128)] = (part[i * ROWS : (i + 1) * ROWS] * gain_k[kz : kz + 1]).astype(BF16)

    fetches["down"].wait()
    low_width = MODEL_WIDTH // GROUPS
    low_part = lax.dot_general(
        normed[:, pl.ds(pl.multiple_of(head * low_width, low_width), low_width)],
        down_v[...].reshape(ADAPTERS * 2 * RANK, low_width), NT, preferred_element_type=F32,
    )
    b_mine = b_buf.at[head]
    b_mine[...] = low_part
    for o in HEAD_PARTNERS:
        send(2, o, b_mine, b_mine)

    fetches["kvw"].wait()
    seq_width = MODEL_WIDTH // SEQ
    keyval_part = jnp.dot(
        normed[:, pl.ds(pl.multiple_of(seq * seq_width, seq_width), seq_width)], kvw_v[...], preferred_element_type=F32
    )
    fetches["qw"].wait()
    query_plain = lax.dot_general(normed[...], qw_v[...], NT, preferred_element_type=F32)
    fetches["qup"].wait()
    fetches["vup"].wait()

    landed(2, b_buf.at[pl.ds(0, GROUPS - 1)])
    low_sum = b_buf[0]
    for k in range(1, GROUPS):
        low_sum = low_sum + b_buf[k]
    low_rank = jnp.where(chosen, low_sum, 0.0).astype(BF16)
    query_delta = jnp.dot(
        low_rank, qup_v[...].reshape(ADAPTERS * 2 * RANK, HALF), preferred_element_type=F32
    )
    query_mine = (query_plain + query_delta).astype(BF16).astype(F32)
    for k in range(4):
        c_msg[k] = jnp.concatenate([query_mine, keyval_part[:, k * HALF : (k + 1) * HALF]], axis=1)
    c_buf[pl.ds(seq, 1)] = c_msg[pl.ds(lax.rem(z, 4), 1)]
    for o in SEQ_PARTNERS:
        send(3, o, c_msg.at[lax.rem(z + o[2], 4)], c_buf.at[seq])
    value_delta = jnp.dot(
        low_rank, vup_v[...].reshape(ADAPTERS * 2 * RANK, HEAD_SIZE), preferred_element_type=F32
    )

    landed(3, c_buf.at[pl.ds(0, SEQ - 1)])
    kv_sum = c_buf[0]
    for k in range(1, SEQ):
        kv_sum = kv_sum + c_buf[k]
    kv_rows[...] = kv_sum
    kv_piece = jnp.broadcast_to(kv_rows[pl.ds(seq // QUADS, 1)], (HEADS, 128))
    for h in range(HEADS):
        former, latter = c_buf[2 * h], c_buf[2 * h + 1]
        first = former * cosine - latter * sine
        second = latter * cosine + former * sine
        turned = jnp.concatenate([first[:, :HALF], second[:, :HALF]], axis=1)
        q_rot[pl.ds(h * ROWS, ROWS)] = turned.astype(BF16).astype(F32)

    fetches["k"].wait()
    fetches["v"].wait()
    where = seq * SPAN + lax.broadcasted_iota(jnp.int32, (HEADS, SPAN), 1)
    lane_h = lax.broadcasted_iota(jnp.int32, (HEADS, 128), 1)
    for b in range(ROWS):
        queries = q_rot[pl.ds(b, HEADS, stride=ROWS)].astype(BF16)
        scores = lax.dot_general(queries, k_v[b], NT, preferred_element_type=F32) * SCORE_SCALE
        valid = where < length_s[b]
        masked = jnp.where(valid, scores, MASKED)
        block_max = jnp.max(masked, axis=1, keepdims=True)
        weights = jnp.where(valid, jnp.exp(masked - block_max), 0.0)
        block_total = jnp.sum(weights, axis=1, keepdims=True)
        block_acc = jnp.dot(weights.astype(BF16), v_v[b], preferred_element_type=F32)
        facts = jnp.where(lane_h < 32, block_max, jnp.where(lane_h < 64, block_total, kv_piece))
        for k in range(QUADS):
            d_msg[b * QUADS + k, pl.ds(0, 4)] = block_acc[4 * k : 4 * k + 4]
            d_msg[b * QUADS + k, pl.ds(4, 4)] = facts[4 * k : 4 * k + 4]
    own = pl.ds(pl.multiple_of(seq * 8, 8), 8)
    d_buf[own] = d_msg[pl.ds(seq, 1)].reshape(8, 128)
    for o in SEQ_PARTNERS:
        send(4, o, d_msg.at[place(o)[0]], d_buf.at[own])
    landed(4, d_buf.at[pl.ds(0, (SEQ - 1) * 8)])

    quarter = [d_buf[pl.ds(8 * k + 4, ROWS, stride=8 * QUADS)] for k in range(4)]
    key_first = quarter[0] * cosine - quarter[1] * sine
    key_second = quarter[1] * cosine + quarter[0] * sine
    key_new = jnp.concatenate([key_first[:, HALF:], key_second[:, HALF:]], axis=1).astype(BF16)
    value_new = (jnp.concatenate([quarter[2][:, HALF:], quarter[3][:, HALF:]], axis=1) + value_delta).astype(BF16)
    kv_ref[:, pl.ds(0, HEAD_SIZE)] = key_new
    kv_ref[:, pl.ds(HEAD_SIZE, HEAD_SIZE)] = value_new

    row, quad = seq // QUADS, lax.rem(seq, QUADS)
    kv_rows[...] = key_new.astype(F32)
    own_key = kv_rows[pl.ds(row, 1)]
    kv_rows[...] = value_new.astype(F32)
    own_value = kv_rows[pl.ds(row, 1)]
    own_queries = q_rot[pl.ds(quad * 4 * ROWS + row, 4, stride=ROWS)]
    self_score = jnp.sum(own_queries * own_key, axis=1, keepdims=True) * SCORE_SCALE
    e_rows = []
    for j in range(4):
        acc = d_buf[pl.ds(j, SEQ, stride=8)]
        facts = d_buf[pl.ds(4 + j, SEQ, stride=8)]
        peaks = jnp.broadcast_to(facts[:, :1], (SEQ, 128))
        own_score = jnp.broadcast_to(self_score[j : j + 1], (1, 128))
        highest = jnp.maximum(jnp.max(peaks, axis=0, keepdims=True), own_score)
        factor = jnp.exp(peaks - highest)
        self_weight = jnp.exp(own_score - highest)
        summed = jnp.sum(factor * facts, axis=0, keepdims=True)
        summed = jnp.broadcast_to(summed[:, 32:33], (1, 128)) + self_weight
        weighted = jnp.sum(factor * acc, axis=0, keepdims=True) + self_weight * own_value
        e_rows.append(weighted / summed)
    attended_own = jnp.concatenate(e_rows + e_rows, axis=0).astype(BF16).astype(F32)
    e_buf[own] = attended_own
    for o in SEQ_PARTNERS:
        send(5, o, e_buf.at[own], e_buf.at[own])
    fetches["ow"].wait()
    landed(5, e_buf.at[pl.ds(0, (SEQ - 1) * 8)])

    attended = jnp.concatenate(
        [e_buf[pl.ds(8 * (h // 4) + h % 4, ROWS, stride=8 * QUADS)] for h in range(HEADS)], axis=1
    ).astype(BF16)
    partial = jnp.dot(attended, ow_v[...], preferred_element_type=F32)
    for k in range(GROUPS):
        tile = partial[:, 128 * (k // 2) : 128 * (k // 2) + 128]
        if k % 2:
            tile = pltpu.roll(tile, HALF, 1)
        f_msg[k] = tile
    f_buf[pl.ds(head, 1)] = f_msg[pl.ds(head, 1)]
    for o in HEAD_PARTNERS:
        send(6, o, f_msg.at[place(o)[1]], f_buf.at[head])
    landed(6, f_buf.at[pl.ds(0, GROUPS - 1)])
    total = f_buf[0]
    for k in range(1, GROUPS):
        total = total + f_buf[k]
    out_ref[...] = total[:, :HALF].astype(BF16)
    for phase, ref in sent:
        pltpu.make_async_copy(ref, ref, send_sem.at[phase]).wait()


def local(
    residual_input,
    norm_gain_vector,
    query_weight,
    key_value_weight,
    output_weight,
    adapter_down_factors,
    query_up_factors,
    value_up_factors,
    adapter_index,
    lengths,
    rotated_key_cache,
    earlier_value_cache,
):
    frequency = np.exp(np.arange(HALF, dtype=np.float64) * (-math.log(ROPE_BASE) / HALF)).astype(np.float32)
    frequency = jnp.asarray(np.concatenate([frequency, frequency])[None, :])
    operands = (
        residual_input,
        norm_gain_vector,
        jnp.transpose(query_weight, (1, 2, 0)).reshape(HALF, MODEL_WIDTH),
        key_value_weight.reshape(MODEL_WIDTH // SEQ, 2 * HEAD_SIZE),
        output_weight.reshape(HEADS * HEAD_SIZE, MODEL_WIDTH // SEQ),
        jnp.transpose(adapter_down_factors, (0, 2, 1)),
        query_up_factors.reshape(ADAPTERS, RANK, HALF),
        value_up_factors.reshape(ADAPTERS, RANK, HEAD_SIZE),
        adapter_index,
        lengths,
        rotated_key_cache.reshape(ROWS, SPAN, HEAD_SIZE),
        earlier_value_cache.reshape(ROWS, SPAN, HEAD_SIZE),
        frequency,
    )
    dma, vmem = pltpu.SemaphoreType.DMA, pltpu.VMEM
    attn_delta, new_keyval = pl.pallas_call(
        kernel,
        out_shape=(
            jax.ShapeDtypeStruct((ROWS, HALF), BF16),
            jax.ShapeDtypeStruct((ROWS, 2 * HEAD_SIZE), BF16),
        ),
        in_specs=[pl.BlockSpec(memory_space=pl.ANY)] * len(operands),
        out_specs=(pl.BlockSpec(memory_space=vmem), pl.BlockSpec(memory_space=vmem)),
        scratch_shapes=[
            vmem((ROWS, HALF), BF16),
            vmem((HALF,), BF16),
            vmem((HALF, MODEL_WIDTH), BF16),
            vmem((MODEL_WIDTH // SEQ, 2 * HEAD_SIZE), BF16),
            vmem((HEADS * HEAD_SIZE, MODEL_WIDTH // SEQ), BF16),
            vmem((ADAPTERS, 2 * RANK, MODEL_WIDTH // GROUPS), BF16),
            vmem((ADAPTERS, 2 * RANK, HALF), BF16),
            vmem((ADAPTERS, 2 * RANK, HEAD_SIZE), BF16),
            pltpu.SMEM((ADAPTERS,), jnp.int32),
            pltpu.SMEM((ROWS,), jnp.int32),
            vmem((ROWS, SPAN, HEAD_SIZE), BF16),
            vmem((ROWS, SPAN, HEAD_SIZE), BF16),
            vmem((1, 128), F32),
            vmem((2 * ROWS, 128), BF16),
            vmem((NZ * NC, 2 * ROWS, 128), BF16),
            vmem((NX * NY, NZ * ROWS + 2 * ROWS, 128), BF16),
            vmem((ROWS, MODEL_WIDTH), BF16),
            vmem((GROUPS, ROWS, ADAPTERS * 2 * RANK), F32),
            vmem((4, ROWS, 128), F32),
            vmem((SEQ, ROWS, 128), F32),
            vmem((HEADS * ROWS, 128), F32),
            vmem((SEQ, 8, 128), F32),
            vmem((SEQ * 8, 128), F32),
            vmem((ROWS, 128), F32),
            vmem((SEQ * 8, 128), F32),
            vmem((GROUPS, ROWS, 128), F32),
            vmem((GROUPS, ROWS, 128), F32),
            dma((13,)),
            dma((7,)),
            dma((7,)),
        ],
        compiler_params=pltpu.CompilerParams(
            collective_id=0, has_side_effects=True, vmem_limit_bytes=62 * 2**20
        ),
        name="decode_attention",
    )(*operands)
    return attn_delta, new_keyval[:, None, :]


def solution(mesh):
    return jax.shard_map(
        local,
        mesh=mesh,
        in_specs=(
            P(None, ("kvseq", "kvhead")),
            P(("kvseq", "kvhead")),
            P(None, "kvhead", "kvseq"),
            P("kvseq", "kvhead", None),
            P("kvhead", None, "kvseq"),
            P(None, "kvhead", None),
            P(None, None, "kvhead", "kvseq"),
            P(None, None, "kvhead", None),
            P(),
            P(),
            P(None, "kvseq", "kvhead", None),
            P(None, "kvseq", "kvhead", None),
        ),
        out_specs=(P(None, ("kvseq", "kvhead")), P(None, "kvhead", None)),
        check_vma=False,
    )
```

time: 456 us -> 56.1 us (0.12)
  blocking collectives: 318 us -> 0 us
  waiting for transfers between devices: 69.1 us -> 0 us
  Pallas kernels: 0 us -> 52.8 us
  other arithmetic: 36 us -> 0 us
  between operations: 14.2 us -> 0.64 us
  matrix products: 10.2 us -> 0 us
    all_gather x4 -> x0, blocking collectives: 166 us -> none  [the longest x1 66.3 us: local(): lax.all_gather(normed_part, ('kvseq', 'kvhead'), axis=1, tiled=True)]
    psum x3 -> x0, blocking collectives: 152 us -> none  [the longest x1 81.4 us: local(): lax.psum(jnp.sum(widened * widened, axis=1), ('kvseq', 'kvhead'))]
    pallas_call x0 -> x1, Pallas kernels: none -> 52.8 us  [local(): pl.pallas_call(kernel, out_shape=(jax.ShapeDtypeStruct((ROWS, HALF), BF16...]
    unnamed x3 -> x0, waiting for transfers between devices: 40.4 us -> none
    add x64 -> x0, other arithmetic: 30.2 us -> none  [the longest x31 29.6 us: combine_parts(): former[2] * weight_a[..., None] + latter[2] * weight_b[..., None]]
    all_gather x1 -> x0, waiting for transfers between devices: 28.7 us -> none  [combined_all(): everything = jax.tree.map(lambda part: lax.all_gather(part, axis), shard)]
    dot_general x8 -> x0, matrix products: 6.97 us -> none  [the longest x1 2.23 us: local(): jnp.dot(normed, query_weight.reshape(MODEL_WIDTH, query_total_width), pre...]
  transfers between devices with their start and end apart: 2 -> 0, of which waited for: 2 -> 0; matrix products, arithmetic and copies ran while one was open for 0% -> 0% of each run, Pallas kernels for 0% -> 0%
where the time goes in v1:
time: 56.1 us; the launch traced here: 55.9 us
  Pallas kernels  52.8 us (94%)
  local copies, waits for them, and re-layouts  2.5 us (4%)
  between operations  0.64 us (1%)
    pallas_call x1, Pallas kernels, local(): pl.pallas_call(kernel, out_shape=(jax.ShapeDtypeStruct((ROWS, HALF), BF16...  52.8 us
    unnamed x2, local copies, waits for them, and re-layouts  2.5 us

profile of v1, /device:TPU:1, one launch (start us, length us, event | category | flops | bytes accessed | tf_op | source)
XLA Modules:
  0.0 55.9 jit_solution(13338963065242442325)
XLA Ops:
  0.6 52.8 %decode_attention.1 = (bf16[8,64]{1,0:T(8,128)(2,1)}, bf16[8,256]{1,0:T(8,128)(2,1)}) custom-call(bf16[8,64]{1,0:T(8,128)(2,1)} %x_hbm.1, bf16[64]{0:T(256)(128)(2,1)} %gain_hbm.1, bf16[64,16384]{1,0:T(8,128)(2,1)} %bitcast.11, bf16[512,256]{1,0:T(8,128)(2,1)} %bitcast.16, bf16[2048,512]{1,0:T(8,128)(2,1)} %bitcast.12, bf16[8,32,2048]{2,1,0:T(8,128)(2,1)} %bitcast.15, ...), custom_call_target="tpu_custom_call" | custom-call | tf_op jit(solution)/shard_map/decode_attention/pallas_call | solution.py:319
  53.4 1.2 %copy.17 = bf16[8,64]{1,0:T(8,128)(2,1)} copy(bf16[8,64]{1,0:T(8,128)(2,1)} %get-tuple-element.8) | data formatting | bytes 2048
  54.6 1.3 %copy.18 = bf16[8,1,256]{2,0,1:T(8,128)(2,1)} copy(bf16[8,1,256]{2,0,1:T(8,128)(2,1)} %bitcast.19) | data formatting | bytes 8192

commit v2 on v1

--- a/solution.py
+++ b/solution.py
@@ -35,6 +35,12 @@
     return min(k, n - k)
 
 
+def added(terms):
+    while len(terms) > 1:
+        terms = [sum(terms[k + 1 : k + 2], terms[k]) for k in range(0, len(terms), 2)]
+    return terms[0]
+
+
 def offsets(xs, ys, zs, cs):
     found = [(x, y, z, c) for x in xs for y in ys for z in zs for c in cs if (x, y, z, c) != (0, 0, 0, 0)]
     return sorted(found, key=lambda o: (-(ring(o[0], NX) + ring(o[1], NY) + ring(o[2], NZ)), -o[3]))
@@ -50,42 +56,51 @@
     x_hbm, gain_hbm, qw_hbm, kvw_hbm, ow_hbm, down_hbm, qup_hbm, vup_hbm, adapter_hbm, length_hbm, k_hbm, v_hbm, freq_hbm,
     out_ref, kv_ref,
     x_v, gain_v, qw_v, kvw_v, ow_v, down_v, qup_v, vup_v, adapter_s, length_s, k_v, v_v, freq_v,
-    z_msg, z_buf, xy_buf, normed, b_buf, c_msg, c_buf, q_rot, d_msg, d_buf, kv_rows, e_buf, f_msg, f_buf,
-    local_sem, send_sem, recv_sem,
+    z_msg, z_buf, xy_buf, sq_buf, group_in, normed, b_buf, c_msg, c_buf, q_rot, d_msg, d_buf, kv_rows, e_buf, f_msg, f_buf,
+    local_sem, send_sem, recv_sem, xy_sem,
 ):
     seq, head = lax.axis_index("kvseq"), lax.axis_index("kvhead")
     x, z = seq // NZ, lax.rem(seq, NZ)
     y, c = head // NC, lax.rem(head, NC)
 
+    at_x = [lax.rem(x + k, NX) for k in range(NX)]
+    at_y = [lax.rem(y + k, NY) for k in range(NY)]
+    at_z = [lax.rem(z + k, NZ) for k in range(NZ)]
+    at_c = [c, 1 - c]
+    at_seq = [[at_x[i] * NZ + at_z[k] for k in range(NZ)] for i in range(NX)]
+    at_head = [[at_y[i] * NC + at_c[k] for k in range(NC)] for i in range(NY)]
+
     def place(o):
-        px, pz = lax.rem(x + o[0], NX), lax.rem(z + o[2], NZ)
-        py, pc = lax.rem(y + o[1], NY), lax.rem(c + o[3], NC)
-        return px * NZ + pz, py * NC + pc
+        return at_seq[o[0]][o[2]], at_head[o[1]][o[3]]
 
     barrier = pltpu.get_barrier_semaphore()
     for o in XY_PARTNERS + Z_PARTNERS:
         pl.semaphore_signal(barrier, inc=1, device_id=place(o), device_id_type=MESH)
 
     fetches = {}
-    for n, (name, src, dst) in enumerate([
-        ("x", x_hbm, x_v), ("gain", gain_hbm, gain_v), ("adapter", adapter_hbm, adapter_s), ("length", length_hbm, length_s),
-        ("freq", freq_hbm, freq_v), ("down", down_hbm, down_v), ("qw", qw_hbm, qw_v), ("kvw", kvw_hbm, kvw_v),
-        ("qup", qup_hbm, qup_v.at[:, pl.ds(0, RANK)]), ("vup", vup_hbm, vup_v.at[:, pl.ds(RANK, RANK)]),
-        ("k", k_hbm, k_v), ("v", v_hbm, v_v), ("ow", ow_hbm, ow_v),
-    ]):
-        fetches[name] = pltpu.make_async_copy(src, dst, local_sem.at[n])
+
+    def fetch(name, src, dst):
+        fetches[name] = pltpu.make_async_copy(src, dst, local_sem.at[len(fetches)])
         fetches[name].start()
 
+    fetch("x", x_hbm, x_v)
+    fetch("gain", gain_hbm, gain_v)
+    fetch("length", length_hbm, length_s)
+    fetch("adapter", adapter_hbm, adapter_s)
+    fetch("freq", freq_hbm, freq_v)
+
     sent = []
 
-    def send(phase, o, src, dst):
+    def send_to(phase, device, src, dst, sem):
         copy = pltpu.make_async_remote_copy(
-            src_ref=src, dst_ref=dst, send_sem=send_sem.at[phase], recv_sem=recv_sem.at[phase],
-            device_id=place(o), device_id_type=MESH,
+            src_ref=src, dst_ref=dst, send_sem=send_sem.at[phase], recv_sem=sem, device_id=device, device_id_type=MESH
         )
         copy.start()
 
-    def landed(phase, ref, sem=None):
+    def send(phase, o, src, dst):
+        send_to(phase, place(o), src, dst, recv_sem.at[phase])
+
+    def landed(phase, ref):
         pltpu.make_async_copy(ref, ref, recv_sem.at[phase]).wait()
         sent.append((phase, ref))
 
@@ -106,6 +121,14 @@
     pl.semaphore_wait(barrier, len(XY_PARTNERS) + len(Z_PARTNERS))
     for o in Z_PARTNERS:
         send(0, o, z_msg, z_buf.at[z * NC + c])
+    fetch("down", down_hbm, down_v)
+    fetch("kvw", kvw_hbm, kvw_v)
+    fetch("qw", qw_hbm, qw_v)
+    fetch("qup", qup_hbm, qup_v.at[:, pl.ds(0, RANK)])
+    fetch("vup", vup_hbm, vup_v.at[:, pl.ds(RANK, RANK)])
+    fetch("k", k_hbm, k_v)
+    fetch("v", v_hbm, v_v)
+    fetch("ow", ow_hbm, ow_v)
 
     fetches["length"].wait()
     fetches["freq"].wait()
@@ -129,20 +152,59 @@
     sub2 = lax.broadcasted_iota(jnp.int32, gain_rows.shape, 0)
     for k in range(NZ):
         gain_rows = jnp.where(sub2 == k, tiles[k][ROWS : ROWS + 1], gain_rows)
-    xy_mine = xy_buf.at[x * NY + y]
+    here = x * NY + y
+    xy_mine = xy_buf.at[here]
+    sq_mine = sq_buf.at[here]
+    sq_mine[...] = added([tile[:ROWS] * tile[:ROWS] for tile in tiles])
+    for o in XY_PARTNERS:
+        send(1, o, sq_mine, sq_mine)
     xy_mine[...] = jnp.concatenate(packed + [gain_rows], axis=0).astype(BF16)
-    for o in XY_PARTNERS:
-        send(1, o, xy_mine, xy_mine)
-    landed(1, xy_buf.at[pl.ds(0, NX * NY - 1)])
-
-    squares = jnp.zeros((2 * ROWS, 128), F32)
-    for k in range(NX * NY):
-        for p in range(NZ // 2):
-            part = xy_buf[k, pl.ds(2 * ROWS * p, 2 * ROWS)].astype(F32)
-            squares = squares + part * part
-    square_sum = jnp.sum(squares[:ROWS] + squares[ROWS:], axis=1, keepdims=True)
+    for ky in range(NY):
+        to_y = lax.rem(x + ky, NY)
+        for kx in (2, 1, 3, 0):
+            there = at_seq[kx][0], to_y * NC + c
+
+            def block_to():
+                send_to(7, there, xy_mine, xy_mine, xy_sem.at[here])
+
+            if kx == 0:
+                pl.when(to_y != y)(block_to)
+            else:
+                block_to()
+    sent.append((7, xy_buf.at[pl.ds(0, NX * NY - 1)]))
+
+    def arrived(k):
+        pltpu.make_async_copy(xy_buf.at[k], xy_buf.at[k], xy_sem.at[k]).wait()
+
+    landed(1, sq_buf.at[pl.ds(0, NX * NY - 1)])
+    square_sum = jnp.sum(added([sq_buf[k] for k in range(NX * NY)]), axis=1, keepdims=True)
     scaling = jnp.broadcast_to(lax.rsqrt(square_sum / MODEL_WIDTH + EPSILON), (ROWS, 128))
     scaling = jnp.concatenate([scaling, scaling], axis=0)
+
+    for ky in range(NY):
+        pl.when(y * NY + ky != here)(lambda ky=ky: arrived(y * NY + ky))
+    for ky in range(NY):
+        k = y * NY + ky
+        gain_k = xy_buf[k, pl.ds(NZ * ROWS, 2 * ROWS)].astype(F32)
+        gain_k = jnp.where(c == 0, gain_k[:4], gain_k[4:8])
+        for p in range(2):
+            start = pl.multiple_of(c * 4 * ROWS + p * 2 * ROWS, 2 * ROWS)
+            part = xy_buf[k, pl.ds(start, 2 * ROWS)].astype(F32) * scaling
+            for i in range(2):
+                tile = (2 * p + i) * NY + ky
+                one = part[i * ROWS : (i + 1) * ROWS] * gain_k[2 * p + i : 2 * p + i + 1]
+                group_in[:, pl.ds(tile * 128, 128)] = one.astype(BF16)
+    fetches["down"].wait()
+    low_width = MODEL_WIDTH // GROUPS
+    b_mine = b_buf.at[head]
+    b_mine[...] = lax.dot_general(
+        group_in[...], down_v[...].reshape(ADAPTERS * 2 * RANK, low_width), NT, preferred_element_type=F32
+    )
+    for o in HEAD_PARTNERS:
+        send(2, o, b_mine, b_mine)
+
+    for k in range(NX * NY):
+        pl.when((k // NY != y) & (k != here))(lambda k=k: arrived(k))
     for k in range(NX * NY):
         kx, ky = k // NY, k % NY
         gain_k = xy_buf[k, pl.ds(NZ * ROWS, 2 * ROWS)].astype(F32)
@@ -153,17 +215,6 @@
                 tile = (kx * NZ + kz) * NY + ky
                 normed[:, pl.ds(tile * 128, 128)] = (part[i * ROWS : (i + 1) * ROWS] * gain_k[kz : kz + 1]).astype(BF16)
 
-    fetches["down"].wait()
-    low_width = MODEL_WIDTH // GROUPS
-    low_part = lax.dot_general(
-        normed[:, pl.ds(pl.multiple_of(head * low_width, low_width), low_width)],
-        down_v[...].reshape(ADAPTERS * 2 * RANK, low_width), NT, preferred_element_type=F32,
-    )
-    b_mine = b_buf.at[head]
-    b_mine[...] = low_part
-    for o in HEAD_PARTNERS:
-        send(2, o, b_mine, b_mine)
-
     fetches["kvw"].wait()
     seq_width = MODEL_WIDTH // SEQ
     keyval_part = jnp.dot(
@@ -171,20 +222,19 @@
     )
     fetches["qw"].wait()
     query_plain = lax.dot_general(normed[...], qw_v[...], NT, preferred_element_type=F32)
+    for k in range(4):
+        c_msg[k] = jnp.concatenate([query_plain, keyval_part[:, k * HALF : (k + 1) * HALF]], axis=1)
     fetches["qup"].wait()
     fetches["vup"].wait()
 
     landed(2, b_buf.at[pl.ds(0, GROUPS - 1)])
-    low_sum = b_buf[0]
-    for k in range(1, GROUPS):
-        low_sum = low_sum + b_buf[k]
+    low_sum = added([b_buf[k] for k in range(GROUPS)])
     low_rank = jnp.where(chosen, low_sum, 0.0).astype(BF16)
     query_delta = jnp.dot(
         low_rank, qup_v[...].reshape(ADAPTERS * 2 * RANK, HALF), preferred_element_type=F32
     )
-    query_mine = (query_plain + query_delta).astype(BF16).astype(F32)
     for k in range(4):
-        c_msg[k] = jnp.concatenate([query_mine, keyval_part[:, k * HALF : (k + 1) * HALF]], axis=1)
+        c_msg[k, :, pl.ds(0, HALF)] = (c_msg[k, :, pl.ds(0, HALF)] + query_delta).astype(BF16).astype(F32)
     c_buf[pl.ds(seq, 1)] = c_msg[pl.ds(lax.rem(z, 4), 1)]
     for o in SEQ_PARTNERS:
         send(3, o, c_msg.at[lax.rem(z + o[2], 4)], c_buf.at[seq])
@@ -193,39 +243,48 @@
     )
 
     landed(3, c_buf.at[pl.ds(0, SEQ - 1)])
-    kv_sum = c_buf[0]
-    for k in range(1, SEQ):
-        kv_sum = kv_sum + c_buf[k]
-    kv_rows[...] = kv_sum
+    kv_rows[...] = added([c_buf[k] for k in range(SEQ)])
     kv_piece = jnp.broadcast_to(kv_rows[pl.ds(seq // QUADS, 1)], (HEADS, 128))
+    halves = [(c_buf[2 * h], c_buf[2 * h + 1]) for h in range(HEADS)]
+    first = [former * cosine - latter * sine for former, latter in halves]
+    second = [latter * cosine + former * sine for former, latter in halves]
+    turned = [jnp.concatenate([first[h][:, :HALF], second[h][:, :HALF]], axis=1) for h in range(HEADS)]
     for h in range(HEADS):
-        former, latter = c_buf[2 * h], c_buf[2 * h + 1]
-        first = former * cosine - latter * sine
-        second = latter * cosine + former * sine
-        turned = jnp.concatenate([first[:, :HALF], second[:, :HALF]], axis=1)
-        q_rot[pl.ds(h * ROWS, ROWS)] = turned.astype(BF16).astype(F32)
+        q_rot[pl.ds(h * ROWS, ROWS)] = turned[h].astype(BF16).astype(F32)
 
     fetches["k"].wait()
     fetches["v"].wait()
     where = seq * SPAN + lax.broadcasted_iota(jnp.int32, (HEADS, SPAN), 1)
     lane_h = lax.broadcasted_iota(jnp.int32, (HEADS, 128), 1)
-    for b in range(ROWS):
-        queries = q_rot[pl.ds(b, HEADS, stride=ROWS)].astype(BF16)
-        scores = lax.dot_general(queries, k_v[b], NT, preferred_element_type=F32) * SCORE_SCALE
-        valid = where < length_s[b]
-        masked = jnp.where(valid, scores, MASKED)
-        block_max = jnp.max(masked, axis=1, keepdims=True)
-        weights = jnp.where(valid, jnp.exp(masked - block_max), 0.0)
-        block_total = jnp.sum(weights, axis=1, keepdims=True)
-        block_acc = jnp.dot(weights.astype(BF16), v_v[b], preferred_element_type=F32)
-        facts = jnp.where(lane_h < 32, block_max, jnp.where(lane_h < 64, block_total, kv_piece))
-        for k in range(QUADS):
-            d_msg[b * QUADS + k, pl.ds(0, 4)] = block_acc[4 * k : 4 * k + 4]
-            d_msg[b * QUADS + k, pl.ds(4, 4)] = facts[4 * k : 4 * k + 4]
+    rows = [lax.rem(2 * x + k, ROWS) for k in (4, 5, 2, 3, 6, 7, 0, 1)]
+    queries = [q_rot[pl.ds(b, HEADS, stride=ROWS)].astype(BF16) for b in rows]
     own = pl.ds(pl.multiple_of(seq * 8, 8), 8)
+    parts = ((range(0, 2), (2,)), (range(2, 6), (1, 3)), (range(6, 8), (0,)))
+    scores = {}
+
+    def score(some):
+        for i in some:
+            scores[i] = lax.dot_general(queries[i], k_v[rows[i]], NT, preferred_element_type=F32)
+
+    score(parts[0][0])
+    for n, (some, turns) in enumerate(parts):
+        if n + 1 < len(parts):
+            score(parts[n + 1][0])
+        valid = {i: where < length_s[rows[i]] for i in some}
+        masked = {i: jnp.where(valid[i], scores[i] * SCORE_SCALE, MASKED) for i in some}
+        block_max = {i: jnp.max(masked[i], axis=1, keepdims=True) for i in some}
+        weights = {i: jnp.where(valid[i], jnp.exp(masked[i] - block_max[i]), 0.0) for i in some}
+        block_total = {i: jnp.sum(weights[i], axis=1, keepdims=True) for i in some}
+        block_acc = {i: jnp.dot(weights[i].astype(BF16), v_v[rows[i]], preferred_element_type=F32) for i in some}
+        for i in some:
+            facts = jnp.where(lane_h < 32, block_max[i], jnp.where(lane_h < 64, block_total[i], kv_piece))
+            for k in range(QUADS):
+                d_msg[rows[i] * QUADS + k, pl.ds(0, 4)] = block_acc[i][4 * k : 4 * k + 4]
+                d_msg[rows[i] * QUADS + k, pl.ds(4, 4)] = facts[4 * k : 4 * k + 4]
+        for o in SEQ_PARTNERS:
+            if o[0] in turns:
+                send(4, o, d_msg.at[at_seq[o[0]][o[2]]], d_buf.at[own])
     d_buf[own] = d_msg[pl.ds(seq, 1)].reshape(8, 128)
-    for o in SEQ_PARTNERS:
-        send(4, o, d_msg.at[place(o)[0]], d_buf.at[own])
     landed(4, d_buf.at[pl.ds(0, (SEQ - 1) * 8)])
 
     quarter = [d_buf[pl.ds(8 * k + 4, ROWS, stride=8 * QUADS)] for k in range(4)]
@@ -243,19 +302,18 @@
     own_value = kv_rows[pl.ds(row, 1)]
     own_queries = q_rot[pl.ds(quad * 4 * ROWS + row, 4, stride=ROWS)]
     self_score = jnp.sum(own_queries * own_key, axis=1, keepdims=True) * SCORE_SCALE
-    e_rows = []
-    for j in range(4):
-        acc = d_buf[pl.ds(j, SEQ, stride=8)]
-        facts = d_buf[pl.ds(4 + j, SEQ, stride=8)]
-        peaks = jnp.broadcast_to(facts[:, :1], (SEQ, 128))
-        own_score = jnp.broadcast_to(self_score[j : j + 1], (1, 128))
-        highest = jnp.maximum(jnp.max(peaks, axis=0, keepdims=True), own_score)
-        factor = jnp.exp(peaks - highest)
-        self_weight = jnp.exp(own_score - highest)
-        summed = jnp.sum(factor * facts, axis=0, keepdims=True)
-        summed = jnp.broadcast_to(summed[:, 32:33], (1, 128)) + self_weight
-        weighted = jnp.sum(factor * acc, axis=0, keepdims=True) + self_weight * own_value
-        e_rows.append(weighted / summed)
+    four = range(4)
+    acc = [d_buf[pl.ds(j, SEQ, stride=8)] for j in four]
+    facts = [d_buf[pl.ds(4 + j, SEQ, stride=8)] for j in four]
+    peaks = [jnp.broadcast_to(facts[j][:, :1], (SEQ, 128)) for j in four]
+    own_score = [jnp.broadcast_to(self_score[j : j + 1], (1, 128)) for j in four]
+    highest = [jnp.maximum(jnp.max(peaks[j], axis=0, keepdims=True), own_score[j]) for j in four]
+    factor = [jnp.exp(peaks[j] - highest[j]) for j in four]
+    self_weight = [jnp.exp(own_score[j] - highest[j]) for j in four]
+    summed = [jnp.sum(factor[j] * facts[j], axis=0, keepdims=True) for j in four]
+    summed = [jnp.broadcast_to(summed[j][:, 32:33], (1, 128)) + self_weight[j] for j in four]
+    weighted = [jnp.sum(factor[j] * acc[j], axis=0, keepdims=True) + self_weight[j] * own_value for j in four]
+    e_rows = [weighted[j] / summed[j] for j in four]
     attended_own = jnp.concatenate(e_rows + e_rows, axis=0).astype(BF16).astype(F32)
     e_buf[own] = attended_own
     for o in SEQ_PARTNERS:
@@ -274,7 +332,7 @@
         f_msg[k] = tile
     f_buf[pl.ds(head, 1)] = f_msg[pl.ds(head, 1)]
     for o in HEAD_PARTNERS:
-        send(6, o, f_msg.at[place(o)[1]], f_buf.at[head])
+        send(6, o, f_msg.at[at_head[o[1]][o[3]]], f_buf.at[head])
     landed(6, f_buf.at[pl.ds(0, GROUPS - 1)])
     total = f_buf[0]
     for k in range(1, GROUPS):
@@ -282,6 +340,15 @@
     out_ref[...] = total[:, :HALF].astype(BF16)
     for phase, ref in sent:
         pltpu.make_async_copy(ref, ref, send_sem.at[phase]).wait()
+
+
+def write_out(delta_ref, keyval_ref, delta_hbm, keyval_hbm, sem):
+    first = pltpu.make_async_copy(delta_ref, delta_hbm, sem.at[0])
+    second = pltpu.make_async_copy(keyval_ref, keyval_hbm, sem.at[1])
+    first.start()
+    second.start()
+    first.wait()
+    second.wait()
 
 
 def local(
@@ -298,7 +365,9 @@
     rotated_key_cache,
     earlier_value_cache,
 ):
-    frequency = np.exp(np.arange(HALF, dtype=np.float64) * (-math.log(ROPE_BASE) / HALF)).astype(np.float32)
+    with jax.ensure_compile_time_eval():
+        frequency = jnp.exp(jnp.arange(HALF, dtype=F32) * (-math.log(ROPE_BASE) / HALF))
+        frequency = np.asarray(frequency)
     frequency = jnp.asarray(np.concatenate([frequency, frequency])[None, :])
     operands = (
         residual_input,
@@ -341,6 +410,8 @@
             vmem((2 * ROWS, 128), BF16),
             vmem((NZ * NC, 2 * ROWS, 128), BF16),
             vmem((NX * NY, NZ * ROWS + 2 * ROWS, 128), BF16),
+            vmem((NX * NY, ROWS, 128), F32),
+            vmem((ROWS, MODEL_WIDTH // GROUPS), BF16),
             vmem((ROWS, MODEL_WIDTH), BF16),
             vmem((GROUPS, ROWS, ADAPTERS * 2 * RANK), F32),
             vmem((4, ROWS, 128), F32),
@@ -353,14 +424,26 @@
             vmem((GROUPS, ROWS, 128), F32),
             vmem((GROUPS, ROWS, 128), F32),
             dma((13,)),
+            dma((8,)),
             dma((7,)),
-            dma((7,)),
+            dma((NX * NY,)),
         ],
         compiler_params=pltpu.CompilerParams(
             collective_id=0, has_side_effects=True, vmem_limit_bytes=62 * 2**20
         ),
         name="decode_attention",
     )(*operands)
+    attn_delta, new_keyval = pl.pallas_call(
+        write_out,
+        out_shape=(
+            jax.ShapeDtypeStruct((ROWS, HALF), BF16),
+            jax.ShapeDtypeStruct((ROWS, 2 * HEAD_SIZE), BF16),
+        ),
+        in_specs=[pl.BlockSpec(memory_space=pl.ANY)] * 2,
+        out_specs=[pl.BlockSpec(memory_space=pl.ANY)] * 2,
+        scratch_shapes=[dma((2,))],
+        name="write_out",
+    )(attn_delta, new_keyval)
     return attn_delta, new_keyval[:, None, :]
 
 

time: 56.1 us -> 51.6 us (0.920)
  local copies, waits for them, and re-layouts: 2.5 us -> 0 us
  Pallas kernels: 52.8 us -> 50.9 us
    pallas_call x1, Pallas kernels: 52.8 us -> 49.6 us  [local(): pl.pallas_call(kernel, out_shape=(jax.ShapeDtypeStruct((ROWS, HALF), BF16...]
    unnamed x2 -> x0, local copies, waits for them, and re-layouts: 2.5 us -> none
    pallas_call x0 -> x1, Pallas kernels: none -> 1.31 us  [local(): pl.pallas_call(write_out, out_shape=(jax.ShapeDtypeStruct((ROWS, HALF), B...]
where the time goes in v2:
time: 51.6 us; the launch traced here: 51.5 us
  Pallas kernels  50.9 us (99%)
  between operations  0.64 us (1%)
    pallas_call x1, Pallas kernels, local(): pl.pallas_call(kernel, out_shape=(jax.ShapeDtypeStruct((ROWS, HALF), BF16...  49.6 us
    pallas_call x1, Pallas kernels, local(): pl.pallas_call(write_out, out_shape=(jax.ShapeDtypeStruct((ROWS, HALF), B...  1.31 us

profile of v2, /device:TPU:1, one launch (start us, length us, event | category | flops | bytes accessed | tf_op | source)
XLA Modules:
  0.0 51.5 jit_solution(2154906761528541242)
XLA Ops:
  0.6 49.6 %decode_attention.1 = (bf16[8,64]{1,0:T(8,128)(2,1)}, bf16[8,256]{1,0:T(8,128)(2,1)}) custom-call(bf16[8,64]{1,0:T(8,128)(2,1)} %x_hbm.1, bf16[64]{0:T(256)(128)(2,1)} %gain_hbm.1, bf16[64,16384]{1,0:T(8,128)(2,1)} %bitcast.11, bf16[512,256]{1,0:T(8,128)(2,1)} %bitcast.16, bf16[2048,512]{1,0:T(8,128)(2,1)} %bitcast.12, bf16[8,32,2048]{2,1,0:T(8,128)(2,1)} %bitcast.15, ...), custom_call_target="tpu_custom_call" | custom-call | tf_op jit(solution)/shard_map/decode_attention/pallas_call | solution.py:388
  50.2 1.3 %write_out.1 = (bf16[8,64]{1,0:T(8,128)(2,1)}, bf16[8,256]{1,0:T(8,128)(2,1)}) custom-call(bf16[8,64]{1,0:T(8,128)(2,1)} %get-tuple-element.6.delta_ref, bf16[8,256]{1,0:T(8,128)(2,1)} %get-tuple-element.7.keyval_ref), custom_call_target="tpu_custom_call" | custom-call | tf_op jit(solution)/shard_map/write_out/pallas_call | solution.py:436

commit v3 on v2

--- a/solution.py
+++ b/solution.py
@@ -20,6 +20,7 @@
 SEQ = NX * NZ
 GROUPS = NY * NC
 QUADS = SEQ // ROWS
+GROUP_WIDTH = MODEL_WIDTH // GROUPS
 
 EPSILON = 1e-05
 ROPE_BASE = 500000.0
@@ -56,7 +57,7 @@
     x_hbm, gain_hbm, qw_hbm, kvw_hbm, ow_hbm, down_hbm, qup_hbm, vup_hbm, adapter_hbm, length_hbm, k_hbm, v_hbm, freq_hbm,
     out_ref, kv_ref,
     x_v, gain_v, qw_v, kvw_v, ow_v, down_v, qup_v, vup_v, adapter_s, length_s, k_v, v_v, freq_v,
-    z_msg, z_buf, xy_buf, sq_buf, group_in, normed, b_buf, c_msg, c_buf, q_rot, d_msg, d_buf, kv_rows, e_buf, f_msg, f_buf,
+    z_msg, z_buf, xy_buf, sq_buf, normed, b_buf, c_msg, c_buf, q_rot, d_msg, d_buf, kv_rows, e_buf, f_msg, f_buf,
     local_sem, send_sem, recv_sem, xy_sem,
 ):
     seq, head = lax.axis_index("kvseq"), lax.axis_index("kvhead")
@@ -142,23 +143,26 @@
     chosen = adapter == lax.broadcasted_iota(jnp.int32, adapter.shape, 1) // (2 * RANK)
     angles = position * freq_v[...]
     cosine, sine = jnp.cos(angles), jnp.sin(angles)
+    signed_sine = jnp.where(lane < HALF, -sine, sine)
     qup_v[:, RANK:, :] = jnp.zeros((ADAPTERS, RANK, HALF), BF16)
     vup_v[:, :RANK, :] = jnp.zeros((ADAPTERS, RANK, HEAD_SIZE), BF16)
 
     landed(0, z_buf.at[pl.ds(0, NZ * NC - 1)])
     tiles = [z_buf[2 * k].astype(F32) + z_buf[2 * k + 1].astype(F32) for k in range(NZ)]
-    packed = [jnp.concatenate([tiles[k][:ROWS], tiles[k + 1][:ROWS]], axis=0) for k in range(0, NZ, 2)]
-    gain_rows = jnp.zeros((2 * ROWS, 128), F32)
-    sub2 = lax.broadcasted_iota(jnp.int32, gain_rows.shape, 0)
-    for k in range(NZ):
-        gain_rows = jnp.where(sub2 == k, tiles[k][ROWS : ROWS + 1], gain_rows)
+    squares = added([tile[:ROWS] * tile[:ROWS] for tile in tiles])
+    facts = squares + pltpu.roll(squares, HALF, 1)
+    half = [jnp.where(c == 0, tiles[k], tiles[k + NZ // 2]) for k in range(NZ // 2)]
+    for k in range(NZ // 2):
+        gain_k = half[k][ROWS : ROWS + 1]
+        facts = jnp.where((sub == 2 * k) & (lane >= HALF), pltpu.roll(gain_k, HALF, 1), facts)
+        facts = jnp.where((sub == 2 * k + 1) & (lane >= HALF), gain_k, facts)
     here = x * NY + y
     xy_mine = xy_buf.at[here]
     sq_mine = sq_buf.at[here]
-    sq_mine[...] = added([tile[:ROWS] * tile[:ROWS] for tile in tiles])
+    sq_mine[...] = facts
     for o in XY_PARTNERS:
         send(1, o, sq_mine, sq_mine)
-    xy_mine[...] = jnp.concatenate(packed + [gain_rows], axis=0).astype(BF16)
+    xy_mine[...] = jnp.concatenate([t[:ROWS] for t in half], axis=0).astype(BF16)
     for ky in range(NY):
         to_y = lax.rem(x + ky, NY)
         for kx in (2, 1, 3, 0):
@@ -177,64 +181,75 @@
         pltpu.make_async_copy(xy_buf.at[k], xy_buf.at[k], xy_sem.at[k]).wait()
 
     landed(1, sq_buf.at[pl.ds(0, NX * NY - 1)])
-    square_sum = jnp.sum(added([sq_buf[k] for k in range(NX * NY)]), axis=1, keepdims=True)
+    square_sum = added([sq_buf[k] for k in range(NX * NY)])
+    square_sum = jnp.sum(jnp.where(lane < HALF, square_sum, 0.0), axis=1, keepdims=True)
     scaling = jnp.broadcast_to(lax.rsqrt(square_sum / MODEL_WIDTH + EPSILON), (ROWS, 128))
     scaling = jnp.concatenate([scaling, scaling], axis=0)
 
-    for ky in range(NY):
-        pl.when(y * NY + ky != here)(lambda ky=ky: arrived(y * NY + ky))
-    for ky in range(NY):
-        k = y * NY + ky
-        gain_k = xy_buf[k, pl.ds(NZ * ROWS, 2 * ROWS)].astype(F32)
-        gain_k = jnp.where(c == 0, gain_k[:4], gain_k[4:8])
-        for p in range(2):
-            start = pl.multiple_of(c * 4 * ROWS + p * 2 * ROWS, 2 * ROWS)
-            part = xy_buf[k, pl.ds(start, 2 * ROWS)].astype(F32) * scaling
-            for i in range(2):
-                tile = (2 * p + i) * NY + ky
-                one = part[i * ROWS : (i + 1) * ROWS] * gain_k[2 * p + i : 2 * p + i + 1]
-                group_in[:, pl.ds(tile * 128, 128)] = one.astype(BF16)
+    def normalize(kx):
+        for ky in range(NY):
+            pl.when(kx * NY + ky != here)(lambda ky=ky: arrived(kx * NY + ky))
+        group = kx * NC + c
+        for ky in range(NY):
+            k = kx * NY + ky
+            gain_odd = sq_buf[k]
+            gain_even = pltpu.roll(gain_odd, HALF, 1)
+            for p in range(2):
+                part = xy_buf[k, pl.ds(p * 2 * ROWS, 2 * ROWS)].astype(F32) * scaling
+                for i in range(2):
+                    n = 2 * p + i
+                    gain_row = jnp.where(lane[:1] < HALF, gain_even[2 * n : 2 * n + 1], gain_odd[2 * n + 1 : 2 * n + 2])
+                    one = part[i * ROWS : (i + 1) * ROWS] * gain_row
+                    normed[group, :, pl.ds((n * NY + ky) * 128, 128)] = one.astype(BF16)
+
+    normalize(y)
     fetches["down"].wait()
-    low_width = MODEL_WIDTH // GROUPS
     b_mine = b_buf.at[head]
     b_mine[...] = lax.dot_general(
-        group_in[...], down_v[...].reshape(ADAPTERS * 2 * RANK, low_width), NT, preferred_element_type=F32
+        normed[head], down_v[...].reshape(ADAPTERS * 2 * RANK, GROUP_WIDTH), NT, preferred_element_type=F32
     )
     for o in HEAD_PARTNERS:
         send(2, o, b_mine, b_mine)
 
-    for k in range(NX * NY):
-        pl.when((k // NY != y) & (k != here))(lambda k=k: arrived(k))
-    for k in range(NX * NY):
-        kx, ky = k // NY, k % NY
-        gain_k = xy_buf[k, pl.ds(NZ * ROWS, 2 * ROWS)].astype(F32)
-        for p in range(NZ // 2):
-            part = xy_buf[k, pl.ds(2 * ROWS * p, 2 * ROWS)].astype(F32) * scaling
-            for i in range(2):
-                kz = 2 * p + i
-                tile = (kx * NZ + kz) * NY + ky
-                normed[:, pl.ds(tile * 128, 128)] = (part[i * ROWS : (i + 1) * ROWS] * gain_k[kz : kz + 1]).astype(BF16)
-
-    fetches["kvw"].wait()
-    seq_width = MODEL_WIDTH // SEQ
-    keyval_part = jnp.dot(
-        normed[:, pl.ds(pl.multiple_of(seq * seq_width, seq_width), seq_width)], kvw_v[...], preferred_element_type=F32
-    )
+    other = (0, 0, 0, 1)
+    send(8, other, normed.at[head], normed.at[head])
+    for k in range(1, NX):
+        normalize(at_y[k])
+        group = at_y[k] * NC + c
+        send(8, other, normed.at[group], normed.at[group])
+
+    def project(group):
+        weight = qw_v[:, pl.ds(pl.multiple_of(group * GROUP_WIDTH, GROUP_WIDTH), GROUP_WIDTH)]
+        return lax.dot_general(normed[group], weight, NT, preferred_element_type=F32)
+
     fetches["qw"].wait()
-    query_plain = lax.dot_general(normed[...], qw_v[...], NT, preferred_element_type=F32)
-    for k in range(4):
-        c_msg[k] = jnp.concatenate([query_plain, keyval_part[:, k * HALF : (k + 1) * HALF]], axis=1)
     fetches["qup"].wait()
     fetches["vup"].wait()
+    fetches["kvw"].wait()
+    query_own = added([project(k * NC + c) for k in range(NX)])
+    c_msg[0, :, pl.ds(0, HALF)] = query_own
+    query_up = qup_v[...].reshape(ADAPTERS * 2 * RANK, HALF)
+    query_up = jnp.concatenate([query_up, query_up], axis=1)
+    landed(8, normed.at[pl.ds(0, NX)])
+    query_plain = added([project(k * NC + 1 - c) for k in range(NX)]) + c_msg[0, :, pl.ds(0, HALF)]
+    seq_width = MODEL_WIDTH // SEQ
+    seq_start = pl.multiple_of(lax.rem(z, 4) * seq_width, seq_width)
+    keyval_part = jnp.dot(
+        normed[x * NC + z // 4, :, pl.ds(seq_start, seq_width)], kvw_v[...], preferred_element_type=F32
+    )
+    query_lanes = lane // HALF == lax.rem(z, 2)
+    plain = jnp.concatenate([query_plain, query_plain], axis=1)
+    for k in range(4):
+        quarter = keyval_part[:, k * HALF : (k + 1) * HALF]
+        c_msg[k] = jnp.where(query_lanes, plain, jnp.concatenate([quarter, quarter], axis=1))
 
     landed(2, b_buf.at[pl.ds(0, GROUPS - 1)])
     low_sum = added([b_buf[k] for k in range(GROUPS)])
     low_rank = jnp.where(chosen, low_sum, 0.0).astype(BF16)
-    query_delta = jnp.dot(
-        low_rank, qup_v[...].reshape(ADAPTERS * 2 * RANK, HALF), preferred_element_type=F32
-    )
+    query_delta = jnp.dot(low_rank, query_up, preferred_element_type=F32)
     for k in range(4):
-        c_msg[k, :, pl.ds(0, HALF)] = (c_msg[k, :, pl.ds(0, HALF)] + query_delta).astype(BF16).astype(F32)
+        message = c_msg[k]
+        c_msg[k] = jnp.where(query_lanes, (message + query_delta).astype(BF16).astype(F32), message)
     c_buf[pl.ds(seq, 1)] = c_msg[pl.ds(lax.rem(z, 4), 1)]
     for o in SEQ_PARTNERS:
         send(3, o, c_msg.at[lax.rem(z + o[2], 4)], c_buf.at[seq])
@@ -243,14 +258,13 @@
     )
 
     landed(3, c_buf.at[pl.ds(0, SEQ - 1)])
-    kv_rows[...] = added([c_buf[k] for k in range(SEQ)])
-    kv_piece = jnp.broadcast_to(kv_rows[pl.ds(seq // QUADS, 1)], (HEADS, 128))
-    halves = [(c_buf[2 * h], c_buf[2 * h + 1]) for h in range(HEADS)]
-    first = [former * cosine - latter * sine for former, latter in halves]
-    second = [latter * cosine + former * sine for former, latter in halves]
-    turned = [jnp.concatenate([first[h][:, :HALF], second[h][:, :HALF]], axis=1) for h in range(HEADS)]
+    pairs = [(c_buf[2 * h], c_buf[2 * h + 1]) for h in range(HEADS)]
+    whole = [jnp.where(lane < HALF, even, odd) for even, odd in pairs]
+    turned = [t * cosine + pltpu.roll(t, HALF, 1) * signed_sine for t in whole]
     for h in range(HEADS):
         q_rot[pl.ds(h * ROWS, ROWS)] = turned[h].astype(BF16).astype(F32)
+    kv_rows[...] = added([even for even, _ in pairs]) + pltpu.roll(added([odd for _, odd in pairs]), HALF, 1)
+    kv_piece = jnp.broadcast_to(kv_rows[pl.ds(seq // QUADS, 1)], (HEADS, 128))
 
     fetches["k"].wait()
     fetches["v"].wait()
@@ -278,16 +292,21 @@
         block_acc = {i: jnp.dot(weights[i].astype(BF16), v_v[rows[i]], preferred_element_type=F32) for i in some}
         for i in some:
             facts = jnp.where(lane_h < 32, block_max[i], jnp.where(lane_h < 64, block_total[i], kv_piece))
-            for k in range(QUADS):
-                d_msg[rows[i] * QUADS + k, pl.ds(0, 4)] = block_acc[i][4 * k : 4 * k + 4]
-                d_msg[rows[i] * QUADS + k, pl.ds(4, 4)] = facts[4 * k : 4 * k + 4]
+            for k in range(2):
+                heads = block_acc[i][8 * k : 8 * k + 8]
+                about = pltpu.roll(facts[8 * k : 8 * k + 8], 4, 0)
+                d_msg[rows[i] * QUADS + 2 * k] = jnp.where(sub < 4, heads, about)
+                d_msg[rows[i] * QUADS + 2 * k + 1] = jnp.where(sub < 4, about, heads)
         for o in SEQ_PARTNERS:
             if o[0] in turns:
                 send(4, o, d_msg.at[at_seq[o[0]][o[2]]], d_buf.at[own])
     d_buf[own] = d_msg[pl.ds(seq, 1)].reshape(8, 128)
     landed(4, d_buf.at[pl.ds(0, (SEQ - 1) * 8)])
 
-    quarter = [d_buf[pl.ds(8 * k + 4, ROWS, stride=8 * QUADS)] for k in range(4)]
+    row, quad = seq // QUADS, lax.rem(seq, QUADS)
+    acc_row = lax.rem(quad, 2) * 4
+    facts_row = 4 - acc_row
+    quarter = [d_buf[pl.ds(8 * k + facts_row, ROWS, stride=8 * QUADS)] for k in range(4)]
     key_first = quarter[0] * cosine - quarter[1] * sine
     key_second = quarter[1] * cosine + quarter[0] * sine
     key_new = jnp.concatenate([key_first[:, HALF:], key_second[:, HALF:]], axis=1).astype(BF16)
@@ -295,7 +314,6 @@
     kv_ref[:, pl.ds(0, HEAD_SIZE)] = key_new
     kv_ref[:, pl.ds(HEAD_SIZE, HEAD_SIZE)] = value_new
 
-    row, quad = seq // QUADS, lax.rem(seq, QUADS)
     kv_rows[...] = key_new.astype(F32)
     own_key = kv_rows[pl.ds(row, 1)]
     kv_rows[...] = value_new.astype(F32)
@@ -303,8 +321,8 @@
     own_queries = q_rot[pl.ds(quad * 4 * ROWS + row, 4, stride=ROWS)]
     self_score = jnp.sum(own_queries * own_key, axis=1, keepdims=True) * SCORE_SCALE
     four = range(4)
-    acc = [d_buf[pl.ds(j, SEQ, stride=8)] for j in four]
-    facts = [d_buf[pl.ds(4 + j, SEQ, stride=8)] for j in four]
+    acc = [d_buf[pl.ds(acc_row + j, SEQ, stride=8)] for j in four]
+    facts = [d_buf[pl.ds(facts_row + j, SEQ, stride=8)] for j in four]
     peaks = [jnp.broadcast_to(facts[j][:, :1], (SEQ, 128)) for j in four]
     own_score = [jnp.broadcast_to(self_score[j : j + 1], (1, 128)) for j in four]
     highest = [jnp.maximum(jnp.max(peaks[j], axis=0, keepdims=True), own_score[j]) for j in four]
@@ -387,10 +405,7 @@
     dma, vmem = pltpu.SemaphoreType.DMA, pltpu.VMEM
     attn_delta, new_keyval = pl.pallas_call(
         kernel,
-        out_shape=(
-            jax.ShapeDtypeStruct((ROWS, HALF), BF16),
-            jax.ShapeDtypeStruct((ROWS, 2 * HEAD_SIZE), BF16),
-        ),
+        out_shape=(vmem((ROWS, HALF), BF16), vmem((ROWS, 2 * HEAD_SIZE), BF16)),
         in_specs=[pl.BlockSpec(memory_space=pl.ANY)] * len(operands),
         out_specs=(pl.BlockSpec(memory_space=vmem), pl.BlockSpec(memory_space=vmem)),
         scratch_shapes=[
@@ -409,10 +424,9 @@
             vmem((1, 128), F32),
             vmem((2 * ROWS, 128), BF16),
             vmem((NZ * NC, 2 * ROWS, 128), BF16),
-            vmem((NX * NY, NZ * ROWS + 2 * ROWS, 128), BF16),
+            vmem((NX * NY, NZ // 2 * ROWS, 128), BF16),
             vmem((NX * NY, ROWS, 128), F32),
-            vmem((ROWS, MODEL_WIDTH // GROUPS), BF16),
-            vmem((ROWS, MODEL_WIDTH), BF16),
+            vmem((GROUPS, ROWS, GROUP_WIDTH), BF16),
             vmem((GROUPS, ROWS, ADAPTERS * 2 * RANK), F32),
             vmem((4, ROWS, 128), F32),
             vmem((SEQ, ROWS, 128), F32),
@@ -424,8 +438,8 @@
             vmem((GROUPS, ROWS, 128), F32),
             vmem((GROUPS, ROWS, 128), F32),
             dma((13,)),
-            dma((8,)),
-            dma((7,)),
+            dma((9,)),
+            dma((9,)),
             dma((NX * NY,)),
         ],
         compiler_params=pltpu.CompilerParams(
@@ -439,9 +453,10 @@
             jax.ShapeDtypeStruct((ROWS, HALF), BF16),
             jax.ShapeDtypeStruct((ROWS, 2 * HEAD_SIZE), BF16),
         ),
-        in_specs=[pl.BlockSpec(memory_space=pl.ANY)] * 2,
+        in_specs=[pl.BlockSpec(memory_space=vmem)] * 2,
         out_specs=[pl.BlockSpec(memory_space=pl.ANY)] * 2,
         scratch_shapes=[dma((2,))],
+        compiler_params=pltpu.CompilerParams(vmem_limit_bytes=2**20),
         name="write_out",
     )(attn_delta, new_keyval)
     return attn_delta, new_keyval[:, None, :]

time: 51.6 us -> 49.9 us (0.967)
  Pallas kernels: 50.9 us -> 49.1 us
    pallas_call x1, Pallas kernels: 49.6 us -> 48.5 us  [local(): pl.pallas_call(kernel, out_shape=(vmem((ROWS, HALF), BF16), vmem((ROWS, 2...]
    pallas_call x1, Pallas kernels: 1.31 us -> 0.62 us  [local(): pl.pallas_call(write_out, out_shape=(jax.ShapeDtypeStruct((ROWS, HALF), B...]
where the time goes in v3:
time: 49.9 us; the launch traced here: 49.8 us
  Pallas kernels  49.1 us (98%)
  between operations  0.64 us (1%)
    pallas_call x1, Pallas kernels, local(): pl.pallas_call(kernel, out_shape=(vmem((ROWS, HALF), BF16), vmem((ROWS, 2...  48.5 us

profile of v3, /device:TPU:1, one launch (start us, length us, event | category | flops | bytes accessed | tf_op | source)
XLA Modules:
  0.0 49.8 jit_solution(13557583481827810953)
XLA Ops:
  0.6 48.5 %decode_attention.1 = (bf16[8,64]{1,0:T(8,128)(2,1)S(1)}, bf16[8,256]{1,0:T(8,128)(2,1)S(1)}) custom-call(bf16[8,64]{1,0:T(8,128)(2,1)} %x_hbm.1, bf16[64]{0:T(256)(128)(2,1)} %gain_hbm.1, bf16[64,16384]{1,0:T(8,128)(2,1)} %bitcast.11, bf16[512,256]{1,0:T(8,128)(2,1)} %bitcast.16, bf16[2048,512]{1,0:T(8,128)(2,1)} %bitcast.12, ...), custom_call_target="tpu_custom_call" | custom-call | tf_op jit(solution)/shard_map/decode_attention/pallas_call | solution.py:406
  49.2 0.6 %write_out.1 = (bf16[8,64]{1,0:T(8,128)(2,1)}, bf16[8,256]{1,0:T(8,128)(2,1)}) custom-call(bf16[8,64]{1,0:T(8,128)(2,1)S(1)} %get-tuple-element.6.delta_ref, bf16[8,256]{1,0:T(8,128)(2,1)S(1)} %get-tuple-element.7.keyval_ref), custom_call_target="tpu_custom_call" | custom-call | tf_op jit(solution)/shard_map/write_out/pallas_call | solution.py:450

commit v4 on v3

--- a/solution.py
+++ b/solution.py
@@ -57,8 +57,8 @@
     x_hbm, gain_hbm, qw_hbm, kvw_hbm, ow_hbm, down_hbm, qup_hbm, vup_hbm, adapter_hbm, length_hbm, k_hbm, v_hbm, freq_hbm,
     out_ref, kv_ref,
     x_v, gain_v, qw_v, kvw_v, ow_v, down_v, qup_v, vup_v, adapter_s, length_s, k_v, v_v, freq_v,
-    z_msg, z_buf, xy_buf, sq_buf, normed, b_buf, c_msg, c_buf, q_rot, d_msg, d_buf, kv_rows, e_buf, f_msg, f_buf,
-    local_sem, send_sem, recv_sem, xy_sem,
+    z_msg, z_buf, xy_buf, sq_buf, normed, b_buf, c_msg, c_buf, up_buf, query_delta, q_rot, d_msg, d_buf, kv_rows, e_buf, f_msg, f_buf,
+    local_sem, send_sem, recv_sem, xy_sem, half_sem,
 ):
     seq, head = lax.axis_index("kvseq"), lax.axis_index("kvhead")
     x, z = seq // NZ, lax.rem(seq, NZ)
@@ -89,6 +89,7 @@
     fetch("length", length_hbm, length_s)
     fetch("adapter", adapter_hbm, adapter_s)
     fetch("freq", freq_hbm, freq_v)
+    fetch("qup", qup_hbm, qup_v)
 
     sent = []
 
@@ -125,8 +126,7 @@
     fetch("down", down_hbm, down_v)
     fetch("kvw", kvw_hbm, kvw_v)
     fetch("qw", qw_hbm, qw_v)
-    fetch("qup", qup_hbm, qup_v.at[:, pl.ds(0, RANK)])
-    fetch("vup", vup_hbm, vup_v.at[:, pl.ds(RANK, RANK)])
+    fetch("vup", vup_hbm, vup_v)
     fetch("k", k_hbm, k_v)
     fetch("v", v_hbm, v_v)
     fetch("ow", ow_hbm, ow_v)
@@ -140,12 +140,10 @@
     for b in range(ROWS):
         position = jnp.where(sub == b, length_s[b].astype(F32), position)
         adapter = jnp.where(sub_wide == b, adapter_s[b], adapter)
-    chosen = adapter == lax.broadcasted_iota(jnp.int32, adapter.shape, 1) // (2 * RANK)
+    chosen = adapter == lax.rem(lax.broadcasted_iota(jnp.int32, adapter.shape, 1), ADAPTERS * RANK) // RANK
     angles = position * freq_v[...]
     cosine, sine = jnp.cos(angles), jnp.sin(angles)
     signed_sine = jnp.where(lane < HALF, -sine, sine)
-    qup_v[:, RANK:, :] = jnp.zeros((ADAPTERS, RANK, HALF), BF16)
-    vup_v[:, :RANK, :] = jnp.zeros((ADAPTERS, RANK, HEAD_SIZE), BF16)
 
     landed(0, z_buf.at[pl.ds(0, NZ * NC - 1)])
     tiles = [z_buf[2 * k].astype(F32) + z_buf[2 * k + 1].astype(F32) for k in range(NZ)]
@@ -177,6 +175,13 @@
                 block_to()
     sent.append((7, xy_buf.at[pl.ds(0, NX * NY - 1)]))
 
+    fetches["qup"].wait()
+    query_up = qup_v[...].reshape(ADAPTERS * RANK, HALF)
+    up_buf[z] = jnp.concatenate([query_up[: ADAPTERS * RANK // 2], query_up[ADAPTERS * RANK // 2 :]], axis=1)
+    for o in Z_PARTNERS:
+        if o[3] == 0:
+            send(9, o, up_buf.at[z], up_buf.at[z])
+
     def arrived(k):
         pltpu.make_async_copy(xy_buf.at[k], xy_buf.at[k], xy_sem.at[k]).wait()
 
@@ -202,36 +207,36 @@
                     one = part[i * ROWS : (i + 1) * ROWS] * gain_row
                     normed[group, :, pl.ds((n * NY + ky) * 128, 128)] = one.astype(BF16)
 
-    normalize(y)
+    other = (0, 0, 0, 1)
+    for k in range(NX):
+        normalize(at_y[k])
+        group = at_y[k] * NC + c
+        send_to(8, place(other), normed.at[group], normed.at[group], half_sem.at[k])
+    sent.append((8, normed.at[pl.ds(0, NX)]))
+
     fetches["down"].wait()
     b_mine = b_buf.at[head]
-    b_mine[...] = lax.dot_general(
-        normed[head], down_v[...].reshape(ADAPTERS * 2 * RANK, GROUP_WIDTH), NT, preferred_element_type=F32
-    )
+    for k in range(2):
+        factors = down_v[:, k * RANK : (k + 1) * RANK].reshape(ADAPTERS * RANK, GROUP_WIDTH)
+        b_mine[:, pl.ds(k * 128, 128)] = lax.dot_general(normed[head], factors, NT, preferred_element_type=F32)
     for o in HEAD_PARTNERS:
         send(2, o, b_mine, b_mine)
-
-    other = (0, 0, 0, 1)
-    send(8, other, normed.at[head], normed.at[head])
-    for k in range(1, NX):
-        normalize(at_y[k])
-        group = at_y[k] * NC + c
-        send(8, other, normed.at[group], normed.at[group])
 
     def project(group):
         weight = qw_v[:, pl.ds(pl.multiple_of(group * GROUP_WIDTH, GROUP_WIDTH), GROUP_WIDTH)]
         return lax.dot_general(normed[group], weight, NT, preferred_element_type=F32)
 
     fetches["qw"].wait()
-    fetches["qup"].wait()
     fetches["vup"].wait()
     fetches["kvw"].wait()
     query_own = added([project(k * NC + c) for k in range(NX)])
     c_msg[0, :, pl.ds(0, HALF)] = query_own
-    query_up = qup_v[...].reshape(ADAPTERS * 2 * RANK, HALF)
-    query_up = jnp.concatenate([query_up, query_up], axis=1)
-    landed(8, normed.at[pl.ds(0, NX)])
-    query_plain = added([project(k * NC + 1 - c) for k in range(NX)]) + c_msg[0, :, pl.ds(0, HALF)]
+    query_parts = [c_msg[0, :, pl.ds(0, HALF)]]
+    for k in range(NX):
+        group = at_y[k] * NC + 1 - c
+        pltpu.make_async_copy(normed.at[group], normed.at[group], half_sem.at[k]).wait()
+        query_parts.append(project(group))
+    query_plain = added(query_parts)
     seq_width = MODEL_WIDTH // SEQ
     seq_start = pl.multiple_of(lax.rem(z, 4) * seq_width, seq_width)
     keyval_part = jnp.dot(
@@ -243,23 +248,35 @@
         quarter = keyval_part[:, k * HALF : (k + 1) * HALF]
         c_msg[k] = jnp.where(query_lanes, plain, jnp.concatenate([quarter, quarter], axis=1))
 
-    landed(2, b_buf.at[pl.ds(0, GROUPS - 1)])
-    low_sum = added([b_buf[k] for k in range(GROUPS)])
-    low_rank = jnp.where(chosen, low_sum, 0.0).astype(BF16)
-    query_delta = jnp.dot(low_rank, query_up, preferred_element_type=F32)
-    for k in range(4):
-        message = c_msg[k]
-        c_msg[k] = jnp.where(query_lanes, (message + query_delta).astype(BF16).astype(F32), message)
     c_buf[pl.ds(seq, 1)] = c_msg[pl.ds(lax.rem(z, 4), 1)]
     for o in SEQ_PARTNERS:
         send(3, o, c_msg.at[lax.rem(z + o[2], 4)], c_buf.at[seq])
+
+    landed(2, b_buf.at[pl.ds(0, GROUPS - 1)])
+    low_sum = added([b_buf[k] for k in range(GROUPS)])
+    low_rank = jnp.where(chosen, low_sum, 0.0)
+    low_query, low_value = low_rank[:, :128], low_rank[:, 128:].astype(BF16)
+    low_query = jnp.concatenate([low_query, pltpu.roll(low_query, HALF, 1)], axis=0)[:, :HALF].astype(BF16)
+    landed(9, up_buf.at[pl.ds(0, NZ - 1)])
+    ring_heads = NZ // 2
+    for h in range(ring_heads):
+        even = jnp.dot(low_query, up_buf[2 * h], preferred_element_type=F32)
+        odd = jnp.dot(low_query, up_buf[2 * h + 1], preferred_element_type=F32)
+        crossed = jnp.where(lane < HALF, odd[:ROWS], even[ROWS:])
+        query_delta[x * ring_heads + h] = jnp.where(lane < HALF, even[:ROWS], odd[ROWS:]) + pltpu.roll(crossed, HALF, 1)
+    ring_delta = query_delta.at[pl.ds(x * ring_heads, ring_heads)]
+    for o in XY_PARTNERS:
+        if o[1] == 0:
+            send(10, o, ring_delta, ring_delta)
     value_delta = jnp.dot(
-        low_rank, vup_v[...].reshape(ADAPTERS * 2 * RANK, HEAD_SIZE), preferred_element_type=F32
+        low_value, vup_v[...].reshape(ADAPTERS * RANK, HEAD_SIZE), preferred_element_type=F32
     )
 
+    landed(10, query_delta.at[pl.ds(0, (NX - 1) * ring_heads)])
     landed(3, c_buf.at[pl.ds(0, SEQ - 1)])
     pairs = [(c_buf[2 * h], c_buf[2 * h + 1]) for h in range(HEADS)]
-    whole = [jnp.where(lane < HALF, even, odd) for even, odd in pairs]
+    whole = [jnp.where(lane < HALF, even, odd) + query_delta[h] for h, (even, odd) in enumerate(pairs)]
+    whole = [t.astype(BF16).astype(F32) for t in whole]
     turned = [t * cosine + pltpu.roll(t, HALF, 1) * signed_sine for t in whole]
     for h in range(HEADS):
         q_rot[pl.ds(h * ROWS, ROWS)] = turned[h].astype(BF16).astype(F32)
@@ -415,8 +432,8 @@
             vmem((MODEL_WIDTH // SEQ, 2 * HEAD_SIZE), BF16),
             vmem((HEADS * HEAD_SIZE, MODEL_WIDTH // SEQ), BF16),
             vmem((ADAPTERS, 2 * RANK, MODEL_WIDTH // GROUPS), BF16),
-            vmem((ADAPTERS, 2 * RANK, HALF), BF16),
-            vmem((ADAPTERS, 2 * RANK, HEAD_SIZE), BF16),
+            vmem((ADAPTERS, RANK, HALF), BF16),
+            vmem((ADAPTERS, RANK, HEAD_SIZE), BF16),
             pltpu.SMEM((ADAPTERS,), jnp.int32),
             pltpu.SMEM((ROWS,), jnp.int32),
             vmem((ROWS, SPAN, HEAD_SIZE), BF16),
@@ -430,6 +447,8 @@
             vmem((GROUPS, ROWS, ADAPTERS * 2 * RANK), F32),
             vmem((4, ROWS, 128), F32),
             vmem((SEQ, ROWS, 128), F32),
+            vmem((NZ, ADAPTERS * RANK // 2, 128), BF16),
+            vmem((HEADS, ROWS, 128), F32),
             vmem((HEADS * ROWS, 128), F32),
             vmem((SEQ, 8, 128), F32),
             vmem((SEQ * 8, 128), F32),
@@ -438,9 +457,10 @@
             vmem((GROUPS, ROWS, 128), F32),
             vmem((GROUPS, ROWS, 128), F32),
             dma((13,)),
-            dma((9,)),
-            dma((9,)),
+            dma((11,)),
+            dma((11,)),
             dma((NX * NY,)),
+            dma((NX,)),
         ],
         compiler_params=pltpu.CompilerParams(
             collective_id=0, has_side_effects=True, vmem_limit_bytes=62 * 2**20

time: 49.9 us -> 47.8 us (0.958)
  Pallas kernels: 49.1 us -> 47 us
    pallas_call x1, Pallas kernels: 48.5 us -> 46.4 us  [local(): pl.pallas_call(kernel, out_shape=(vmem((ROWS, HALF), BF16), vmem((ROWS, 2...]
where the time goes in v4:
time: 47.8 us; the launch traced here: 47.7 us
  Pallas kernels  47 us (98%)
  between operations  0.64 us (1%)
    pallas_call x1, Pallas kernels, local(): pl.pallas_call(kernel, out_shape=(vmem((ROWS, HALF), BF16), vmem((ROWS, 2...  46.4 us

profile of v4, /device:TPU:1, one launch (start us, length us, event | category | flops | bytes accessed | tf_op | source)
XLA Modules:
  0.0 47.7 jit_solution(2187723687418187019)
XLA Ops:
  0.6 46.4 %decode_attention.1 = (bf16[8,64]{1,0:T(8,128)(2,1)S(1)}, bf16[8,256]{1,0:T(8,128)(2,1)S(1)}) custom-call(bf16[8,64]{1,0:T(8,128)(2,1)} %x_hbm.1, bf16[64]{0:T(256)(128)(2,1)} %gain_hbm.1, bf16[64,16384]{1,0:T(8,128)(2,1)} %bitcast.11, bf16[512,256]{1,0:T(8,128)(2,1)} %bitcast.16, bf16[2048,512]{1,0:T(8,128)(2,1)} %bitcast.12, ...), custom_call_target="tpu_custom_call" | custom-call | tf_op jit(solution)/shard_map/decode_attention/pallas_call | solution.py:423
  47.0 0.6 %write_out.1 = (bf16[8,64]{1,0:T(8,128)(2,1)}, bf16[8,256]{1,0:T(8,128)(2,1)}) custom-call(bf16[8,64]{1,0:T(8,128)(2,1)S(1)} %get-tuple-element.6.delta_ref, bf16[8,256]{1,0:T(8,128)(2,1)S(1)} %get-tuple-element.7.keyval_ref), custom_call_target="tpu_custom_call" | custom-call | tf_op jit(solution)/shard_map/write_out/pallas_call | solution.py:470

commit v5 on v4

--- a/solution.py
+++ b/solution.py
@@ -42,9 +42,13 @@
     return terms[0]
 
 
+def far_first(o):
+    return -(ring(o[0], NX) + ring(o[1], NY) + ring(o[2], NZ)), -o[3]
+
+
 def offsets(xs, ys, zs, cs):
     found = [(x, y, z, c) for x in xs for y in ys for z in zs for c in cs if (x, y, z, c) != (0, 0, 0, 0)]
-    return sorted(found, key=lambda o: (-(ring(o[0], NX) + ring(o[1], NY) + ring(o[2], NZ)), -o[3]))
+    return sorted(found, key=far_first)
 
 
 Z_PARTNERS = offsets([0], [0], range(NZ), range(NC))
@@ -75,7 +79,7 @@
         return at_seq[o[0]][o[2]], at_head[o[1]][o[3]]
 
     barrier = pltpu.get_barrier_semaphore()
-    for o in XY_PARTNERS + Z_PARTNERS:
+    for o in sorted(XY_PARTNERS + Z_PARTNERS, key=far_first):
         pl.semaphore_signal(barrier, inc=1, device_id=place(o), device_id_type=MESH)
 
     fetches = {}
@@ -161,18 +165,8 @@
     for o in XY_PARTNERS:
         send(1, o, sq_mine, sq_mine)
     xy_mine[...] = jnp.concatenate([t[:ROWS] for t in half], axis=0).astype(BF16)
-    for ky in range(NY):
-        to_y = lax.rem(x + ky, NY)
-        for kx in (2, 1, 3, 0):
-            there = at_seq[kx][0], to_y * NC + c
-
-            def block_to():
-                send_to(7, there, xy_mine, xy_mine, xy_sem.at[here])
-
-            if kx == 0:
-                pl.when(to_y != y)(block_to)
-            else:
-                block_to()
+    for o in XY_PARTNERS:
+        send_to(7, place(o), xy_mine, xy_mine, xy_sem.at[here])
     sent.append((7, xy_buf.at[pl.ds(0, NX * NY - 1)]))
 
     fetches["qup"].wait()
@@ -208,9 +202,10 @@
                     normed[group, :, pl.ds((n * NY + ky) * 128, 128)] = one.astype(BF16)
 
     other = (0, 0, 0, 1)
+    by_distance = [at_x[k] for k in (0, 1, 3, 2)]
     for k in range(NX):
-        normalize(at_y[k])
-        group = at_y[k] * NC + c
+        normalize(by_distance[k])
+        group = by_distance[k] * NC + c
         send_to(8, place(other), normed.at[group], normed.at[group], half_sem.at[k])
     sent.append((8, normed.at[pl.ds(0, NX)]))
 
@@ -233,7 +228,7 @@
     c_msg[0, :, pl.ds(0, HALF)] = query_own
     query_parts = [c_msg[0, :, pl.ds(0, HALF)]]
     for k in range(NX):
-        group = at_y[k] * NC + 1 - c
+        group = by_distance[k] * NC + 1 - c
         pltpu.make_async_copy(normed.at[group], normed.at[group], half_sem.at[k]).wait()
         query_parts.append(project(group))
     query_plain = added(query_parts)
@@ -359,15 +354,22 @@
     attended = jnp.concatenate(
         [e_buf[pl.ds(8 * (h // 4) + h % 4, ROWS, stride=8 * QUADS)] for h in range(HEADS)], axis=1
     ).astype(BF16)
-    partial = jnp.dot(attended, ow_v[...], preferred_element_type=F32)
-    for k in range(GROUPS):
-        tile = partial[:, 128 * (k // 2) : 128 * (k // 2) + 128]
-        if k % 2:
-            tile = pltpu.roll(tile, HALF, 1)
-        f_msg[k] = tile
+    width = MODEL_WIDTH // SEQ // 2
+    for far in (True, False):
+        pair = 1 - y // 2 if far else y // 2
+        columns = pl.ds(pl.multiple_of(pair * width, width), width)
+        partial = jnp.dot(attended, ow_v[:, columns], preferred_element_type=F32)
+        for k in range(GROUPS // 2):
+            tile = partial[:, 128 * (k // 2) : 128 * (k // 2) + 128]
+            if k % 2:
+                tile = pltpu.roll(tile, HALF, 1)
+            f_msg[pair * (GROUPS // 2) + k] = tile
+        same, crossed = pair * 2 + lax.rem(y, 2), pair * 2 + 1 - lax.rem(y, 2)
+        targets = [(same, 1), (same, 0), (crossed, 1), (crossed, 0)] if far else [(crossed, 1), (crossed, 0), (same, 1)]
+        for to_y, to_c in targets:
+            to = to_y * NC + at_c[to_c]
+            send_to(6, (seq, to), f_msg.at[to], f_buf.at[head], recv_sem.at[6])
     f_buf[pl.ds(head, 1)] = f_msg[pl.ds(head, 1)]
-    for o in HEAD_PARTNERS:
-        send(6, o, f_msg.at[at_head[o[1]][o[3]]], f_buf.at[head])
     landed(6, f_buf.at[pl.ds(0, GROUPS - 1)])
     total = f_buf[0]
     for k in range(1, GROUPS):
@@ -449,11 +451,11 @@
             vmem((SEQ, ROWS, 128), F32),
             vmem((NZ, ADAPTERS * RANK // 2, 128), BF16),
             vmem((HEADS, ROWS, 128), F32),
-            vmem((HEADS * ROWS, 128), F32),
+            vmem((HEADS * ROWS + 8, 128), F32),
             vmem((SEQ, 8, 128), F32),
-            vmem((SEQ * 8, 128), F32),
+            vmem((SEQ * 8 + 32, 128), F32),
             vmem((ROWS, 128), F32),
-            vmem((SEQ * 8, 128), F32),
+            vmem((SEQ * 8 + 32, 128), F32),
             vmem((GROUPS, ROWS, 128), F32),
             vmem((GROUPS, ROWS, 128), F32),
             dma((13,)),

time: 47.8 us -> 47.5 us (level)
  no operation moved by 1% of the time
where the time goes in v5:
time: 47.5 us; the launch traced here: 47.4 us
  Pallas kernels  46.8 us (99%)
  between operations  0.64 us (1%)
    pallas_call x1, Pallas kernels, local(): pl.pallas_call(kernel, out_shape=(vmem((ROWS, HALF), BF16), vmem((ROWS, 2...  46.1 us

profile of v5, /device:TPU:1, one launch (start us, length us, event | category | flops | bytes accessed | tf_op | source)
XLA Modules:
  0.0 47.4 jit_solution(5832595789660326684)
XLA Ops:
  0.6 46.1 %decode_attention.1 = (bf16[8,64]{1,0:T(8,128)(2,1)S(1)}, bf16[8,256]{1,0:T(8,128)(2,1)S(1)}) custom-call(bf16[8,64]{1,0:T(8,128)(2,1)} %x_hbm.1, bf16[64]{0:T(256)(128)(2,1)} %gain_hbm.1, bf16[64,16384]{1,0:T(8,128)(2,1)} %bitcast.11, bf16[512,256]{1,0:T(8,128)(2,1)} %bitcast.16, bf16[2048,512]{1,0:T(8,128)(2,1)} %bitcast.12, ...), custom_call_target="tpu_custom_call" | custom-call | tf_op jit(solution)/shard_map/decode_attention/pallas_call | solution.py:425
  46.8 0.6 %write_out.1 = (bf16[8,64]{1,0:T(8,128)(2,1)}, bf16[8,256]{1,0:T(8,128)(2,1)}) custom-call(bf16[8,64]{1,0:T(8,128)(2,1)S(1)} %get-tuple-element.6.delta_ref, bf16[8,256]{1,0:T(8,128)(2,1)S(1)} %get-tuple-element.7.keyval_ref), custom_call_target="tpu_custom_call" | custom-call | tf_op jit(solution)/shard_map/write_out/pallas_call | solution.py:472
